TPU v7x, 32 devices: a whole 2x2x4 slice. The times are simulated.
32 devices in a mesh: row: 8 (over y, x, core), col: 4 (over z).
Axes of the slice: x: 2, y: 2, z: 4, core: 2. Of those that a mesh axis runs over, the one named last changes fastest.
Arguments:
- hidden: bfloat16 [64, 2048], P('row', 'col'), may hold values from -60 to 60
- queries: bfloat16 [64, 4096], P('row'), may hold values from -6 to 6
- new_kv: bfloat16 [64, 2, 2048], P('row'), may hold values from -12 to 12
- prompt_kv: bfloat16 [8, 2, 1024, 2048], P('row', None, 'col'), may hold values from -180 to 180
- suffix_kv: bfloat16 [64, 2, 128, 2048], P('row', None, 'col'), may hold values from -12 to 12
- lengths: int32 [64], P('row'), may hold values from 1 to 128, as said below
- w_out: bfloat16 [4096, 2048], P(None, 'col'), may hold values from -0.375 to 0.375
- moe_gain: bfloat16 [2048], P('col'), may hold values from 0.099609375 to 1.8984375
- w_router: bfloat16 [2048, 8], P('col'), may hold values from -0.5 to 0.5
- expert_weights: bfloat16 [8, 5632, 3, 2048], P(None, 'row', None, 'col'), may hold values from -0.25 to 0.25
- old_lines: int32 [8, 5632], replicated, may hold values from 0 to 5631, as said below
- new_lines: int32 [8, 5632], replicated, may hold values from 0 to 5631, as said below
- routes: int32 [64, 2], replicated, may hold values from 0 to 7, all different within a row
Outputs:
- layer_out: float32 [64, 2048], P('row', 'col')
- moved_weights: bfloat16 [8, 5632, 3, 2048], P(None, 'row', None, 'col')
Inputs may be any that keep to these rules, and one draw needn't show every extreme that they name: `lengths`: some sequence has all 128 slots filled. `old_lines`: each row is a permutation of the hidden units of one expert; stored lines [j * 704, (j + 1) * 704) lie on row index j. `new_lines`: each row is a permutation of the hidden units of one expert. Counting all experts together, exactly 704 of the lines that one row index holds under old_lines are held by each row index under new_lines. `routes`: the two experts of a token differ.
All inputs are finite; a program needn't handle non-finite values.
Results may differ from a plain program's by a relative error of at most 0.04.
Values may be sent and summed in bfloat16 or wider, within the bound.
No kernel may reach another device: no remote copies, remote signals or barrier semaphores. Data moves between devices by JAX's collectives and lax.ppermute only.
A program may use at most 128 MiB of HBM per device.

v0:
```python
import jax
import jax.numpy as jnp
from jax import lax
from jax.sharding import PartitionSpec as P

D = 2048
KVH = 16
HD = 128
REP = 2


norm_eps = 1e-06
neg_big = -1e30


def joined(part, axis, combine):
    gathered = jax.tree.map(lambda a: lax.all_gather(a, axis), part)

    def take(source):
        return jax.tree.map(lambda a: lax.dynamic_index_in_dim(a, source, 0, False), gathered)

    return lax.fori_loop(
        1, lax.axis_size(axis), lambda source, state: combine(state, take(source)), take(0)
    )


def merge_partial(earlier, following):
    highest_a, totals_a, mixture_a = earlier
    highest_b, totals_b, mixture_b = following
    highest = jnp.maximum(highest_a, highest_b)
    factor_a = jnp.exp(highest_a - highest)
    factor_b = jnp.exp(highest_b - highest)
    return (
        highest,
        totals_a * factor_a + totals_b * factor_b,
        mixture_a * factor_a[..., None] + mixture_b * factor_b[..., None],
    )


def attend(queries, new_kv, prompt_kv, suffix_kv, lengths):
    seq_count = queries.shape[0]
    prompt_rows = prompt_kv.shape[2]
    suffix_rows = suffix_kv.shape[2]
    col_index = lax.axis_index("col")
    query_heads = queries.reshape(seq_count, KVH, REP, HD)
    prompt_keys = prompt_kv[0, 0].reshape(prompt_rows, KVH, HD)
    prompt_values = prompt_kv[0, 1].reshape(prompt_rows, KVH, HD)
    suffix_keys = suffix_kv[:, 0].reshape(seq_count, suffix_rows, KVH, HD)
    suffix_values = suffix_kv[:, 1].reshape(seq_count, suffix_rows, KVH, HD)
    own_keys = new_kv[:, 0].reshape(seq_count, KVH, HD)
    own_values = new_kv[:, 1].reshape(seq_count, KVH, HD)
    score_scale = HD ** (-0.5)
    prompt_scores = (
        jnp.einsum("skgd,pkd->skgp", query_heads, prompt_keys, preferred_element_type=jnp.float32)
        * score_scale
    )
    suffix_scores = (
        jnp.einsum("skgd,spkd->skgp", query_heads, suffix_keys, preferred_element_type=jnp.float32)
        * score_scale
    )
    own_scores = (
        jnp.einsum("skgd,skd->skg", query_heads, own_keys, preferred_element_type=jnp.float32)
        * score_scale
    )
    positions = col_index * suffix_rows + jnp.arange(suffix_rows, dtype=jnp.int32)
    live_slots = (positions[None, :] < lengths[:, None])[:, None, None, :]
    holder = col_index == 0
    suffix_scores = jnp.where(live_slots, suffix_scores, neg_big)
    own_scores = jnp.where(holder, own_scores, neg_big)
    highest = jnp.maximum(
        jnp.maximum(jnp.max(prompt_scores, axis=-1), jnp.max(suffix_scores, axis=-1)), own_scores
    )
    prompt_weights = jnp.exp(prompt_scores - highest[..., None])
    suffix_weights = jnp.where(live_slots, jnp.exp(suffix_scores - highest[..., None]), 0.0)
    own_weights = jnp.where(holder, jnp.exp(own_scores - highest), 0.0)
    totals = jnp.sum(prompt_weights, axis=-1) + jnp.sum(suffix_weights, axis=-1) + own_weights
    mixture = jnp.einsum(
        "skgp,pkd->skgd",
        prompt_weights.astype(jnp.bfloat16),
        prompt_values,
        preferred_element_type=jnp.float32,
    )
    mixture = mixture + jnp.einsum(
        "skgp,spkd->skgd",
        suffix_weights.astype(jnp.bfloat16),
        suffix_values,
        preferred_element_type=jnp.float32,
    )
    own_rounded = lax.optimization_barrier(own_weights.astype(jnp.bfloat16)).astype(jnp.float32)
    mixture = mixture + own_rounded[..., None] * own_values.astype(jnp.float32)[:, :, None, :]
    highest, totals, mixture = joined((highest, totals, mixture), "col", merge_partial)
    return (mixture / totals[..., None]).astype(jnp.bfloat16).reshape(seq_count, -1)


def inverse_rows(table):
    expert_count, full_width = table.shape
    row_ids = jnp.broadcast_to(jnp.arange(expert_count, dtype=jnp.int32)[:, None], table.shape)
    slot_ids = jnp.broadcast_to(jnp.arange(full_width, dtype=jnp.int32)[None, :], table.shape)
    return jnp.zeros_like(table).at[row_ids, table].set(slot_ids)


def migrate(expert_weights, old_lines, new_lines):
    row_count = lax.axis_size("row")
    row_index = lax.axis_index("row")
    expert_count, line_count, three_parts, width_col = expert_weights.shape
    full_width = old_lines.shape[1]
    unit_count = expert_count * line_count
    per_peer = unit_count // row_count
    inverse_old = inverse_rows(old_lines)
    inverse_new = inverse_rows(new_lines)
    held_ids = lax.dynamic_slice_in_dim(old_lines, row_index * line_count, line_count, 1)
    target_slots = jnp.take_along_axis(inverse_new, held_ids, axis=1)
    expert_ids = jnp.arange(expert_count, dtype=jnp.int32)[:, None]
    sort_keys = (
        target_slots // line_count * (expert_count * full_width)
        + expert_ids * full_width
        + target_slots
    )
    sort_order = jnp.argsort(sort_keys.reshape(-1))
    flat_units = expert_weights.reshape(unit_count, three_parts, width_col)
    outgoing = flat_units[sort_order].reshape(row_count, per_peer, three_parts, width_col)
    arrived = lax.all_to_all(outgoing, "row", split_axis=0, concat_axis=0, tiled=True).reshape(
        unit_count, three_parts, width_col
    )
    wanted_ids = lax.dynamic_slice_in_dim(new_lines, row_index * line_count, line_count, 1)
    anchor_rows = (jnp.take_along_axis(inverse_old, wanted_ids, axis=1) // line_count).reshape(-1)
    anchor_hits = (anchor_rows[:, None] == jnp.arange(row_count, dtype=jnp.int32)[None, :]).astype(
        jnp.int32
    )
    rank_within = jnp.sum(jnp.cumsum(anchor_hits, axis=0) * anchor_hits, axis=1) - 1
    arrived_slot = anchor_rows * per_peer + rank_within
    return arrived[arrived_slot].reshape(expert_count, line_count, three_parts, width_col)


def activate(summed, router_sum, square_sum, chosen):
    inverse_rms = lax.rsqrt(square_sum / D + norm_eps)
    logits = router_sum * inverse_rms[:, None]
    expert_hits = chosen[:, :, None] == jnp.arange(logits.shape[1], dtype=jnp.int32)[None, None, :]
    selected = jnp.sum(jnp.where(expert_hits, logits[:, None, :], 0.0), axis=-1)
    gates = jax.nn.softmax(selected, axis=-1)
    gate_part = summed[:, :, 0] * inverse_rms[:, None, None]
    up_part = summed[:, :, 1] * inverse_rms[:, None, None]
    activated = (jax.nn.silu(gate_part) * up_part).astype(jnp.bfloat16)
    return (gates, activated)


def local(
    hidden,
    queries,
    new_kv,
    prompt_kv,
    suffix_kv,
    lengths,
    w_out,
    moe_gain,
    w_router,
    expert_weights,
    old_lines,
    new_lines,
    routes,
):
    moved_weights = migrate(expert_weights, old_lines, new_lines)
    attended = attend(queries, new_kv, prompt_kv, suffix_kv, lengths)
    projected = jnp.dot(attended, w_out, preferred_element_type=jnp.float32)
    h_mid = (hidden.astype(jnp.float32) + projected).astype(jnp.bfloat16)
    h_float = h_mid.astype(jnp.float32)
    scaled = (h_float * moe_gain.astype(jnp.float32)[None, :]).astype(jnp.bfloat16)
    squares = jnp.sum(h_float * h_float, axis=1)
    every_token, every_square = (
        lax.all_gather(scaled, "row", axis=0, tiled=True),
        lax.all_gather(squares.astype(jnp.bfloat16), "row", axis=0, tiled=True).astype(
            squares.dtype
        ),
    )
    token_total = every_token.shape[0]
    router_part = jnp.dot(every_token, w_router, preferred_element_type=jnp.float32)
    gate_up = jnp.einsum(
        "td,efjd->etjf",
        every_token,
        expert_weights[:, :, :2, :],
        preferred_element_type=jnp.float32,
    )
    picked = gate_up[routes, jnp.arange(token_total, dtype=jnp.int32)[:, None]]
    summed, router_sum, square_sum = lax.psum((picked, router_part, every_square), "col")
    gates, activated = activate(summed, router_sum, square_sum, routes)
    down_lines = expert_weights[:, :, 2, :]
    top_count = routes.shape[1]
    every_expert = jnp.einsum(
        "tkf,efd->etkd", activated, down_lines, preferred_element_type=jnp.float32
    )
    chosen_out = every_expert[
        routes,
        jnp.arange(hidden.shape[0] * lax.axis_size("row"), dtype=jnp.int32)[:, None],
        jnp.arange(top_count, dtype=jnp.int32)[None, :],
    ]
    mixed = lax.psum_scatter(
        jnp.sum(chosen_out * gates[:, :, None], axis=1), "row", scatter_dimension=0, tiled=True
    )
    layer_out = h_float + mixed
    return (layer_out, moved_weights)


def solution(mesh):
    return jax.shard_map(
        local,
        mesh=mesh,
        in_specs=(
            P("row", "col"),
            P("row", None),
            P("row", None, None),
            P("row", None, "col", None),
            P("row", None, "col", None),
            P("row"),
            P(None, "col"),
            P("col"),
            P("col", None),
            P(None, "row", None, "col"),
            P(),
            P(),
            P(),
        ),
        out_specs=(P("row", "col"), P(None, "row", None, "col")),
        check_vma=False,
    )
```

profile of v0, /device:TPU:0, one launch (start us, length us, event | category | flops | bytes accessed | tf_op | source)
XLA Modules:
  0.0 923.4 jit_solution(3157186968136141646)
XLA Ops:
  12.5 165.0 %scatter_custom_fusion = s32[45056]{0:T(1024)S(1)} fusion(s32[45056]{0:T(1024)S(1)} %reshape.244, s32[45056]{0:T(1024)S(1)} %reshape.246, s32[]{:T(128)} %constant.115.clone.1), kind=kCustom, calls=%fused_computation.71 | custom fusion | bytes 180228
  177.6 34.6 %gather_fusion.4 = s32[5632]{0:T(1024)S(1)} fusion(s32[8,5632]{1,0:T(8,128)S(1)} %reshape.197, s32[5632]{0:T(1024)S(1)} %reshape.287), kind=kCustom, calls=%fused_computation.clone | custom fusion | bytes 90112 | tf_op jit(solution)/shard_map/jit(take_along_axis)/gather | solution.py:112
  213.1 6.8 sort.17
  219.9 8.2 copy.180
  228.2 73.8 %copy.185 = bf16[5632,3,512]{2,1,0:T(4,128)(2,1)} copy(bf16[5632,3,512]{2,0,1:T(8,128)(2,1)S(1)} %bitcast.144) | data formatting | bytes 34603008 | tf_op jit(solution)/shard_map/reshape | solution.py:120
  301.9 34.1 %gather_fusion.2 = bf16[5632,3,512]{2,1,0:T(4,128)(2,1)} fusion(bf16[5632,3,512]{2,1,0:T(4,128)(2,1)} %copy.185, s32[6144]{0:T(1024)S(1)} %pad_clamp_fusion.1), kind=kCustom, calls=%fused_computation.4 | custom fusion | bytes 34625536 | tf_op jit(solution)/shard_map/gather | solution.py:121
  336.0 18.8 %copy.186 = bf16[8,704,3,512]{3,1,2,0:T(8,128)(2,1)} copy(bf16[8,704,3,512]{3,2,1,0:T(4,128)(2,1)} %bitcast.141) | data formatting | bytes 34603008 | tf_op jit(solution)/shard_map/reshape | solution.py:121
  354.9 5.8 all-to-all-start
  360.9 1.7 fusion.61
  364.4 2.7 fusion.62
  367.1 1.5 copy.203
  372.9 14.8 %all-gather.1 = f32[32,16,2]{1,2,0:T(2,128)S(1)} all-gather(f32[8,16,2]{1,2,0:T(2,128)S(1)} %copy.167), channel_id=3, replica_groups=mesh['row'=8,'col'=4] {'col'}, dimensions={0}, use_global_device_ids=true | all-gather | bytes 5120 | tf_op jit(solution)/shard_map/all_gather | solution.py:17
  393.3 15.8 %all-gather.2 = f32[32,16,2,128]{3,0,2,1:T(8,128)S(1)} all-gather(f32[8,16,2,128]{3,0,2,1:T(8,128)S(1)} %fusion.14), channel_id=4, replica_groups=mesh['row'=8,'col'=4] {'col'}, dimensions={0}, use_global_device_ids=true | all-gather | bytes 655360 | tf_op jit(solution)/shard_map/all_gather | solution.py:17
  409.1 13.1 %all-gather = f32[32,16,2]{1,2,0:T(2,128)S(1)} all-gather(f32[8,16,2]{1,2,0:T(2,128)S(1)} %copy.162), channel_id=2, replica_groups=mesh['row'=8,'col'=4] {'col'}, dimensions={0}, use_global_device_ids=true | all-gather | bytes 5120 | tf_op jit(solution)/shard_map/all_gather | solution.py:17
  422.3 3.4 while.19
  426.0 2.9 multiply_reduce_fusion.3
  429.0 125.1 %all_gather.30 = bf16[64,512]{1,0:T(8,128)(2,1)S(1)} all-gather(bf16[8,512]{1,0:T(8,128)(2,1)S(1)} %get-tuple-element.269), channel_id=1, replica_groups=mesh['row'=8,'col'=4] {'row'}, dimensions={0}, use_global_device_ids=true | all-gather | bytes 73728 | tf_op jit(solution)/shard_map/all_gather | solution.py:170
  554.1 6.2 fusion.7
  560.3 2.4 copy.178
  563.1 2.5 gather_fusion
  565.5 2.2 copy.179
  567.8 165.5 %scatter_custom_fusion.1 = s32[45056]{0:T(1024)S(1)} fusion(s32[45056]{0:T(1024)S(1)} %reshape.250, s32[45056]{0:T(1024)} %copy-done.2, s32[]{:T(128)} %constant.115.clone.1), kind=kCustom, calls=%fused_computation.69 | custom fusion | bytes 180736
  733.4 34.6 %gather_fusion.5 = s32[5632]{0:T(1024)S(1)} fusion(s32[8,5632]{1,0:T(8,128)S(1)} %reshape.201, s32[5632]{0:T(1024)S(1)} %reshape.292), kind=kCustom, calls=%fused_computation.1.clone | custom fusion | bytes 90112 | tf_op jit(solution)/shard_map/jit(take_along_axis)/gather | solution.py:126
  769.1 2.4 reduce-window.6
  773.6 13.2 %all-reduce = bf16[64]{0:T(256)(128)(2,1)S(1)} all-reduce(bf16[64]{0:T(256)(128)(2,1)S(1)} %dynamic-update-slice), channel_id=1, replica_groups=mesh['row'=8,'col'=4] {'row'}, use_global_device_ids=true, to_apply=%add | all-reduce | flops 64 | bytes 256
  786.9 13.0 %all-reduce.1 = (f32[64]{0:T(128)S(1)}, f32[64,8]{0,1:T(8,128)S(1)}) all-reduce(bf16[64]{0:T(256)(128)(2,1)S(1)} %all-reduce, f32[64,8]{0,1:T(8,128)S(1)} %fusion.65), channel_id=1, replica_groups=mesh['row'=8,'col'=4] {'col'}, use_global_device_ids=true, to_apply=%region_8.9 | all-reduce | flops 576 | bytes 4480 | tf_op jit(solution)/shard_map/psum | solution.py:184
  800.6 4.0 fusion.10
  804.5 1.6 copy.182
  808.7 29.7 %reduce-scatter.2.cloned.1.call-done = f32[8,512]{1,0:T(8,128)} async-done(((f32[64,512]{1,0:T(8,128)}), f32[8,512]{1,0:T(8,128)}) %reduce-scatter.2.cloned.1.call-update) | async-done | bytes 16400 | tf_op jit(solution)/shard_map/reduce_scatter | solution.py:196
  839.7 23.8 %copy.187 = bf16[8,704,3,512]{3,2,1,0:T(4,128)(2,1)} copy(bf16[8,704,3,512]{3,1,2,0:T(8,128)(2,1)} %all-to-all-done) | data formatting | bytes 34603008 | tf_op jit(solution)/shard_map/all_to_all | solution.py:122
  863.6 34.1 %gather_fusion.3 = bf16[5632,3,512]{2,1,0:T(4,128)(2,1)} fusion(bf16[5632,3,512]{2,1,0:T(4,128)(2,1)} %bitcast.142, s32[6144]{0:T(1024)S(1)} %pad_clamp_fusion), kind=kCustom, calls=%fused_computation.5 | custom fusion | bytes 34625536 | tf_op jit(solution)/shard_map/gather | solution.py:132
  897.7 18.8 %copy.189 = bf16[8,704,3,512]{3,1,2,0:T(8,128)(2,1)} copy(bf16[8,704,3,512]{3,2,1,0:T(4,128)(2,1)} %bitcast.143) | data formatting | bytes 34603008
  (132 shorter events, 29.4 us)
Async XLA Ops:
  7.2 779.6 %copy-start = (bf16[512,8]{0,1:T(8,128)(2,1)S(1)}, bf16[512,8]{0,1:T(8,128)(2,1)}, u32[]{:S(2)}) copy-start(bf16[512,8]{0,1:T(8,128)(2,1)} %param.25) | copy-start | bytes 24580
  10.8 201.3 %copy-start.2 = (s32[45056]{0:T(1024)}, s32[45056]{0:T(1024)S(1)}, u32[]{:S(2)}) copy-start(s32[45056]{0:T(1024)S(1)} %reshape.246) | copy-start | bytes 540676
  354.9 484.9 %all-to-all-start = ((bf16[8,704,3,512]{3,1,2,0:T(8,128)(2,1)}), bf16[8,704,3,512]{3,1,2,0:T(8,128)(2,1)}, u32[]{:S(2)}, u32[]{:S(2)}) async-start(bf16[8,704,3,512]{3,1,2,0:T(8,128)(2,1)} %copy.186), calls=%async_computation.1 | async-start | bytes 34603008 | tf_op jit(solution)/shard_map/all_to_all | solution.py:122
  360.6 439.9 %all-reduce.4.cloned.1.call-start = ((), (), s32[]{:S(2)}) async-start(), calls=%async_computation.2 | async-start | bytes 1572864 | tf_op jit(solution)/shard_map/psum | solution.py:184
  360.9 2.0 copy-start.9
  360.9 2.1 copy-start.3
  363.0 8.1 copy-start.6
  371.1 1.8 copy-start.4
  409.0 17.0 %copy-start.8 = (bf16[512]{0:T(512)(128)(2,1)S(1)}, bf16[512]{0:T(512)(128)(2,1)}, u32[]{:S(2)}) copy-start(bf16[512]{0:T(512)(128)(2,1)} %param.24) | copy-start | bytes 3076
  409.0 17.0 %copy-start.5 = (bf16[8,512]{1,0:T(8,128)(2,1)S(1)}, bf16[8,512]{1,0:T(8,128)(2,1)}, u32[]{:S(2)}) copy-start(bf16[8,512]{1,0:T(8,128)(2,1)} %param.17) | copy-start | bytes 24580
  560.3 2.5 copy-start.7
  562.8 5.0 copy-start.1
  567.7 270.7 %reduce-scatter.2.cloned.1.call-start = ((), (), s32[]{:S(2)}) async-start(), calls=%async_computation.3 | async-start | bytes 147456 | tf_op jit(solution)/shard_map/reduce_scatter | solution.py:196
  733.4 38.7 %copy-start.10 = (u32[32]{0:T(128)S(1)}, u32[32]{0:T(128)}, u32[]{:S(2)}) copy-start(u32[32]{0:T(128)} %constant.209) | copy-start | bytes 388
Sparse Core Ops, SparseCore 0:
  567.8 44.8 all-reduce.3
  808.7 29.6 reduce-scatter.1
where the time goes:
time: 925 us; the launch traced here: 923 us
  local copies, waits for them, and re-layouts  634 us (69%)
  blocking collectives  195 us (21%)
  waiting for transfers between devices  29.8 us (3%)
  other arithmetic  24.9 us (3%)
  matrix products  18.5 us (2%)
  between operations  15.3 us (2%)
    unnamed x35, local copies, waits for them, and re-layouts  361 us
    all_gather x1, blocking collectives, local(): lax.all_gather(scaled, 'row', axis=0, tiled=True)  125 us
    reshape x1, local copies, waits for them, and re-layouts, migrate(): flat_units = expert_weights.reshape(unit_count, three_parts, width_col)  73.8 us
    all_gather x3, blocking collectives, joined(): gathered = jax.tree.map(lambda a: lax.all_gather(a, axis), part)  43.7 us
    gather x3, local copies, waits for them, and re-layouts, migrate(): target_slots = jnp.take_along_axis(inverse_new, held_ids, axis=1)  34.7 us
    gather x3, local copies, waits for them, and re-layouts, migrate(): jnp.take_along_axis(inverse_old, wanted_ids, axis=1) // line_count  34.7 us
    gather x1, local copies, waits for them, and re-layouts, migrate(): flat_units[sort_order].reshape(row_count, per_peer, three_parts, width_col)  34.1 us
    gather x1, local copies, waits for them, and re-layouts, migrate(): arrived[arrived_slot]  34.1 us
  transfers between devices with their start and end apart: 3, of which 1 were waited for; matrix products, arithmetic and copies ran while one was open for 27% of the time, Pallas kernels for 0%

commit v1 on v0

v1 whole, which is shorter than its diff:
```python
import functools

import jax
import jax.numpy as jnp
from jax import lax
from jax.experimental import pallas as pl
from jax.experimental.pallas import tpu as pltpu
from jax.sharding import PartitionSpec as P

KVH = 16
HD = 128
REP = 2
TILE = 16
LANES = 128

norm_eps = 1e-06
neg_big = -1e30
VMEM_LIMIT = 48 * 1024 * 1024


def up_to(value, unit):
    return -(-value // unit) * unit


def iota(shape, axis):
    return lax.broadcasted_iota(jnp.int32, shape, axis)


def ones_where(mask):
    return jnp.where(mask, 1.0, 0.0).astype(jnp.bfloat16)


def params():
    return pltpu.CompilerParams(vmem_limit_bytes=VMEM_LIMIT)


def find_slots(table_row, id_row):
    full = table_row.shape[1]
    ids = id_row.shape[1]
    high_count = up_to(-(-full // 64), 16)
    table_high = ones_where(iota((high_count, full), 0) == (table_row >> 6))
    half = iota((LANES, full), 0)
    slot = iota((LANES, full), 1)
    value = jnp.where(half < 64, slot >> 7, slot & 127).astype(jnp.float32)
    table_low = jnp.where((half & 63) == (table_row & 63), value, 0.0).astype(jnp.bfloat16)
    square = lax.dot_general(
        table_low, table_high, (((1,), (1,)), ((), ())), preferred_element_type=jnp.float32
    )
    id_high = ones_where(iota((high_count, ids), 0) == (id_row >> 6))
    spread = jnp.dot(square.astype(jnp.bfloat16), id_high, preferred_element_type=jnp.float32)
    chosen = jnp.where((iota((LANES, ids), 0) & 63) == (id_row & 63), spread, 0.0)
    high = jnp.sum(chosen[:64], axis=0, keepdims=True)
    low = jnp.sum(chosen[64:], axis=0, keepdims=True)
    return high * 128.0 + low


def segment_plan(counts, experts, rows):
    starts = []
    running = jnp.zeros((rows, LANES), jnp.float32)
    for e in range(experts):
        starts.append(running)
        running = running + counts[e * rows : (e + 1) * rows]
    start = jnp.concatenate(starts, axis=0)
    lead = jnp.floor(start * (1.0 / TILE))
    tail = jnp.floor((start + counts + (TILE - 1.0)) * (1.0 / TILE))
    tiles = jnp.where(counts > 0.0, tail - lead, 0.0)
    pairs = experts * rows
    line = iota((pairs, pairs), 0)
    column = iota((pairs, pairs), 1)
    earlier = ones_where((line // rows == column // rows) & (column < line))
    base = jnp.dot(earlier, tiles.astype(jnp.bfloat16), preferred_element_type=jnp.float32)
    return start, lead, tiles, base


def write_plan(plan_ref, start, lead, tiles, base):
    shared = start - lead * TILE
    for n, part in enumerate((lead, tiles, base, shared)):
        plan_ref[n] = part.astype(jnp.int32)


def outgoing_kernel(lines, rows, new_ref, held_ref, stack_ref, plan_ref):
    experts = new_ref.shape[0]
    width = held_ref.shape[1]
    real = iota((1, width), 1) < lines
    hits = []
    for e in range(experts):
        slots = find_slots(new_ref[e : e + 1, :], held_ref[e : e + 1, :])
        peer = jnp.floor((slots + 0.5) * (1.0 / lines)).astype(jnp.int32)
        hits.append(jnp.where((iota((rows, width), 0) == peer) & real, 1.0, 0.0))
    hits = jnp.concatenate(hits, axis=0)
    until = ones_where(iota((width, width), 0) <= iota((width, width), 1))
    ranks = jnp.dot(hits.astype(jnp.bfloat16), until, preferred_element_type=jnp.float32)
    counts = jnp.broadcast_to(jnp.sum(hits, axis=1, keepdims=True), (experts * rows, LANES))
    start, lead, tiles, base = segment_plan(counts, experts, rows)
    write_plan(plan_ref, start, lead, tiles, base)
    offset = (base * TILE + start - lead * TILE - 1.0)[:, :1]
    placed = hits * (ranks + offset)
    for e in range(experts):
        row = jnp.sum(placed[e * rows : (e + 1) * rows], axis=0, keepdims=True)
        stack_ref[e] = jnp.where(real, row, -1.0).astype(jnp.int32)


def incoming_kernel(lines, rows, old_ref, wanted_ref, stack_ref, plan_ref):
    experts = old_ref.shape[0]
    width = wanted_ref.shape[1]
    real = iota((1, width), 1) < lines
    held_at = []
    hits = []
    for e in range(experts):
        slots = find_slots(old_ref[e : e + 1, :], wanted_ref[e : e + 1, :])
        held_at.append(jnp.where(real, slots, 1e9))
        peer = jnp.floor((slots + 0.5) * (1.0 / lines)).astype(jnp.int32)
        hits.append(jnp.where((iota((rows, width), 0) == peer) & real, 1.0, 0.0))
    hits = jnp.concatenate(hits, axis=0)
    counts = jnp.broadcast_to(jnp.sum(hits, axis=1, keepdims=True), (experts * rows, LANES))
    start, lead, tiles, base = segment_plan(counts, experts, rows)
    write_plan(plan_ref, start, lead, tiles, base)
    blank = jnp.zeros((LANES - experts, width), jnp.float32)
    columns = jnp.transpose(jnp.concatenate(held_at + [blank], axis=0))
    rows_out = []
    for e in range(experts):
        mine = slice(e * rows, (e + 1) * rows)
        before = jnp.where(columns[:, e : e + 1] < held_at[e], 1.0, 0.0)
        rank = jnp.sum(before, axis=0, keepdims=True)
        ahead = jnp.zeros((1, LANES), jnp.float32)
        firsts = []
        for r in range(rows):
            firsts.append(ahead)
            ahead = ahead + counts[e * rows + r : e * rows + r + 1]
        first = jnp.concatenate(firsts, axis=0)
        offset = (base[mine] * TILE + start[mine] - lead[mine] * TILE - first)[:, :1]
        rows_out.append(jnp.sum(hits[mine] * (rank + offset), axis=0, keepdims=True))
    stack_ref[...] = jnp.transpose(jnp.concatenate(rows_out + [blank], axis=0))


def pack_kernel(rows, plan_ref, place_ref, lines_ref, out_ref, stage_ref):
    e = pl.program_id(0)
    pairs = pl.num_programs(0) * rows
    deep, _ = stage_ref.shape
    lines = lines_ref.shape[2]
    place = place_ref[0][:, :lines]
    onehot = ones_where(iota((deep, lines), 0) == place)
    stage_ref[...] = jnp.dot(
        onehot, lines_ref[0, 0], preferred_element_type=jnp.float32
    ).astype(jnp.bfloat16)

    def one_peer(d, carry):
        k = e * rows + d
        lead = plan_ref[k]
        tiles = plan_ref[pairs + k]
        base = plan_ref[2 * pairs + k]
        shared = plan_ref[3 * pairs + k] > 0

        def source(t):
            return stage_ref[pl.ds(pl.multiple_of((base + t) * TILE, TILE), TILE), :]

        def target(t):
            return pl.ds(pl.multiple_of((lead + t) * TILE, TILE), TILE)

        @pl.when((tiles > 0) & shared)
        def _():
            out_ref[d, target(0), :] = out_ref[d, target(0), :] + source(0)

        @pl.when((tiles > 0) & jnp.logical_not(shared))
        def _():
            out_ref[d, target(0), :] = source(0)

        def put(t, c):
            out_ref[d, target(t), :] = source(t)
            return c

        return lax.fori_loop(1, tiles, put, carry)

    lax.fori_loop(0, rows, one_peer, 0)


def unpack_kernel(rows, plan_ref, place_ref, block_ref, *rest):
    out_ref, stage_ref = rest[-2:]
    e = pl.program_id(0)
    pairs = pl.num_programs(0) * rows
    deep, _ = stage_ref.shape
    lines = out_ref.shape[2]

    @pl.when(e == 0)
    def _():
        stage_ref[...] = jnp.zeros_like(stage_ref)

    def one_peer(s, carry):
        k = e * rows + s
        lead = plan_ref[k]
        tiles = plan_ref[pairs + k]
        base = plan_ref[2 * pairs + k]

        def put(t, c):
            here = pl.ds(pl.multiple_of((base + t) * TILE, TILE), TILE)
            there = pl.ds(pl.multiple_of((lead + t) * TILE, TILE), TILE)
            stage_ref[here, :] = block_ref[s, there, :]
            return c

        return lax.fori_loop(0, tiles, put, carry)

    lax.fori_loop(0, rows, one_peer, 0)
    place = jnp.where(iota((lines, LANES), 1) == e, place_ref[:lines, :], 0.0)
    place = jnp.sum(place, axis=1, keepdims=True).astype(jnp.int32)
    onehot = ones_where(iota((lines, deep), 1) == place)
    out_ref[0, 0] = jnp.dot(
        onehot, stage_ref[...], preferred_element_type=jnp.float32
    ).astype(jnp.bfloat16)


def call_plan(kernel, name, table, ids, lines, rows, transposed):
    experts, width = ids.shape
    stack = (
        jax.ShapeDtypeStruct((width, LANES), jnp.float32)
        if transposed
        else jax.ShapeDtypeStruct((experts, 1, width), jnp.int32)
    )
    stack, plan = pl.pallas_call(
        functools.partial(kernel, lines, rows),
        out_shape=(stack, jax.ShapeDtypeStruct((4, experts * rows, LANES), jnp.int32)),
        compiler_params=params(),
        cost_estimate=pl.CostEstimate(
            flops=20 * experts * table.shape[1] * 256,
            bytes_accessed=8 * table.size,
            transcendentals=0,
        ),
        name=name,
    )(table, ids)
    return stack, plan[:, :, 0].reshape(-1)


def pack(expert_lines, place, plan, part, rows, block_rows, deep):
    experts, _, lines, width = expert_lines.shape
    return pl.pallas_call(
        functools.partial(pack_kernel, rows),
        grid_spec=pltpu.PrefetchScalarGridSpec(
            num_scalar_prefetch=1,
            grid=(experts,),
            in_specs=[
                pl.BlockSpec((1, 1, place.shape[2]), lambda e, plan: (e, 0, 0)),
                pl.BlockSpec((1, 1, lines, width), lambda e, plan: (e, part, 0, 0)),
            ],
            out_specs=pl.BlockSpec((rows, block_rows, width), lambda e, plan: (0, 0, 0)),
            scratch_shapes=[pltpu.VMEM((deep, width), jnp.bfloat16)],
        ),
        out_shape=jax.ShapeDtypeStruct((rows, block_rows, width), jnp.bfloat16),
        compiler_params=params(),
        cost_estimate=pl.CostEstimate(
            flops=2 * experts * deep * lines * width,
            bytes_accessed=4 * experts * lines * width,
            transcendentals=0,
        ),
        name="pack_lines",
    )(plan, place, expert_lines)


def unpack(arrived, place, plan, part, shape, deep, previous):
    experts, _, lines, width = shape
    rows, block_rows, _ = arrived.shape
    in_specs = [
        pl.BlockSpec(place.shape, lambda e, plan: (0, 0)),
        pl.BlockSpec((rows, block_rows, width), lambda e, plan: (0, 0, 0)),
    ]
    operands = [plan, place, arrived]
    aliases = {}
    if previous is not None:
        in_specs.append(pl.BlockSpec(memory_space=pl.ANY))
        operands.append(previous)
        aliases = {3: 0}
    return pl.pallas_call(
        functools.partial(unpack_kernel, rows),
        grid_spec=pltpu.PrefetchScalarGridSpec(
            num_scalar_prefetch=1,
            grid=(experts,),
            in_specs=in_specs,
            out_specs=pl.BlockSpec((1, 1, lines, width), lambda e, plan: (e, part, 0, 0)),
            scratch_shapes=[pltpu.VMEM((deep, width), jnp.bfloat16)],
        ),
        out_shape=jax.ShapeDtypeStruct(shape, jnp.bfloat16),
        input_output_aliases=aliases,
        compiler_params=params(),
        cost_estimate=pl.CostEstimate(
            flops=2 * experts * deep * lines * width,
            bytes_accessed=4 * experts * lines * width,
            transcendentals=0,
        ),
        name="unpack_lines",
    )(*operands)


def own_ids(table, lines, width):
    mine = lax.dynamic_slice_in_dim(table, lax.axis_index("row") * lines, lines, 1)
    return jnp.pad(mine, ((0, 0), (0, width - lines)), constant_values=-1)


def migrate(expert_lines, old_lines, new_lines):
    rows = lax.axis_size("row")
    experts, parts, lines, width = expert_lines.shape
    padded = up_to(lines, LANES)
    block_rows = up_to(experts * lines // rows, TILE)
    deep = up_to(lines + 2 * (TILE - 1) * rows, TILE)
    out_place, out_plan = call_plan(
        outgoing_kernel, "outgoing_plan", new_lines, own_ids(old_lines, lines, padded),
        lines, rows, False,
    )
    in_place, in_plan = call_plan(
        incoming_kernel, "incoming_plan", old_lines, own_ids(new_lines, lines, padded),
        lines, rows, True,
    )
    moved = None
    packed = [
        pack(expert_lines, out_place, out_plan, part, rows, block_rows, deep)
        for part in range(parts)
    ]
    arrived = [lax.all_to_all(block, "row", split_axis=0, concat_axis=0, tiled=True) for block in packed]
    for part in range(parts):
        moved = unpack(
            arrived[part], in_place, in_plan, part, expert_lines.shape, up_to(deep, LANES), moved
        )
    return moved


def from_peer(block, axis, offset):
    size = lax.axis_size(axis)
    return lax.ppermute(block, axis, [(i, i ^ offset) for i in range(size)])


def attend(queries, new_kv, prompt_kv, suffix_kv, lengths):
    seq_count = queries.shape[0]
    prompt_rows = prompt_kv.shape[2]
    suffix_rows = suffix_kv.shape[2]
    col_index = lax.axis_index("col")
    query_heads = queries.reshape(seq_count, KVH, REP, HD)
    prompt_keys = prompt_kv[0, 0].reshape(prompt_rows, KVH, HD)
    prompt_values = prompt_kv[0, 1].reshape(prompt_rows, KVH, HD)
    suffix_keys = suffix_kv[:, 0].reshape(seq_count, suffix_rows, KVH, HD)
    suffix_values = suffix_kv[:, 1].reshape(seq_count, suffix_rows, KVH, HD)
    own_keys = new_kv[:, 0].reshape(seq_count, KVH, HD)
    own_values = new_kv[:, 1].reshape(seq_count, KVH, HD)
    score_scale = HD ** (-0.5)
    prompt_scores = (
        jnp.einsum("skgd,pkd->skgp", query_heads, prompt_keys, preferred_element_type=jnp.float32)
        * score_scale
    )
    suffix_scores = (
        jnp.einsum("skgd,spkd->skgp", query_heads, suffix_keys, preferred_element_type=jnp.float32)
        * score_scale
    )
    own_scores = (
        jnp.einsum("skgd,skd->skg", query_heads, own_keys, preferred_element_type=jnp.float32)
        * score_scale
    )
    positions = col_index * suffix_rows + jnp.arange(suffix_rows, dtype=jnp.int32)
    live_slots = (positions[None, :] < lengths[:, None])[:, None, None, :]
    holder = col_index == 0
    suffix_scores = jnp.where(live_slots, suffix_scores, neg_big)
    own_scores = jnp.where(holder, own_scores, neg_big)
    highest = jnp.maximum(
        jnp.maximum(jnp.max(prompt_scores, axis=-1), jnp.max(suffix_scores, axis=-1)), own_scores
    )
    prompt_weights = jnp.exp(prompt_scores - highest[..., None])
    suffix_weights = jnp.where(live_slots, jnp.exp(suffix_scores - highest[..., None]), 0.0)
    own_weights = jnp.where(holder, jnp.exp(own_scores - highest), 0.0)
    totals = jnp.sum(prompt_weights, axis=-1) + jnp.sum(suffix_weights, axis=-1) + own_weights
    mixture = jnp.einsum(
        "skgp,pkd->skgd",
        prompt_weights.astype(jnp.bfloat16),
        prompt_values,
        preferred_element_type=jnp.float32,
    )
    mixture = mixture + jnp.einsum(
        "skgp,spkd->skgd",
        suffix_weights.astype(jnp.bfloat16),
        suffix_values,
        preferred_element_type=jnp.float32,
    )
    own_rounded = lax.optimization_barrier(own_weights.astype(jnp.bfloat16)).astype(jnp.float32)
    mixture = mixture + own_rounded[..., None] * own_values.astype(jnp.float32)[:, :, None, :]
    heads = KVH * REP
    bundle = jnp.concatenate(
        [
            mixture.reshape(seq_count, heads * HD),
            highest.reshape(seq_count, heads),
            totals.reshape(seq_count, heads),
            jnp.zeros((seq_count, LANES - 2 * heads), jnp.float32),
        ],
        axis=1,
    )
    bundles = [bundle] + [from_peer(bundle, "col", o) for o in range(1, lax.axis_size("col"))]
    every = jnp.stack(bundles)
    mixtures = every[:, :, : heads * HD].reshape(-1, seq_count, heads, HD)
    peaks = every[:, :, heads * HD : heads * HD + heads]
    sums = every[:, :, heads * HD + heads : heads * HD + 2 * heads]
    factors = jnp.exp(peaks - jnp.max(peaks, axis=0))
    total = jnp.sum(sums * factors, axis=0)
    mixed = jnp.sum(mixtures * factors[..., None], axis=0)
    return (mixed / total[..., None]).astype(jnp.bfloat16).reshape(seq_count, heads * HD)


def gate_up_kernel(me_ref, h_ref, gain_ref, router_ref, routes_ref, gate_ref, up_ref, out_ref, acc_ref):
    e = pl.program_id(0)
    tokens = h_ref.shape[0]
    lines = gate_ref.shape[2]
    padded = out_ref.shape[3]
    h = h_ref[...].astype(jnp.float32)
    scaled = (h * gain_ref[...].astype(jnp.float32)).astype(jnp.bfloat16)

    @pl.when(e == 0)
    def _():
        acc_ref[...] = jnp.zeros_like(acc_ref)

    against = (((1,), (1,)), ((), ()))
    gate = lax.dot_general(scaled, gate_ref[0, 0], against, preferred_element_type=jnp.float32)
    up = lax.dot_general(scaled, up_ref[0, 0], against, preferred_element_type=jnp.float32)
    for k in range(routes_ref.shape[1]):
        chosen = routes_ref[:, k : k + 1] == e
        acc_ref[2 * k, :, :lines] += jnp.where(chosen, gate, 0.0)
        acc_ref[2 * k + 1, :, :lines] += jnp.where(chosen, up, 0.0)

    @pl.when(e == pl.num_programs(0) - 1)
    def _():
        last = padded - LANES
        shift = lines - last
        experts = pl.num_programs(0)
        extra = jnp.dot(scaled, router_ref[...], preferred_element_type=jnp.float32)
        lane = iota((tokens, LANES), 1)
        square = jnp.sum(h * h, axis=1, keepdims=True)
        extra = jnp.where(lane == shift + experts, square, extra)
        high = extra.astype(jnp.bfloat16).astype(jnp.float32)
        low = extra - high
        acc_ref[0, :, last:] += jnp.where(lane >= shift, high, 0.0)
        acc_ref[1, :, last:] += jnp.where(lane >= shift, low, 0.0)
        peers, _, share, _ = out_ref.shape
        me = me_ref[0]
        for o in range(peers):
            begin = pl.multiple_of((me ^ o) * share, share)
            out_ref[o] = acc_ref[:, pl.ds(begin, share), :].astype(jnp.bfloat16)


def activate_kernel(lines, experts, model_width, routes_ref, *refs):
    out_ref = refs[-1]
    summed = refs[0][...].astype(jnp.float32)
    for ref in refs[1:-1]:
        summed = summed + ref[...].astype(jnp.float32)
    _, share, padded = summed.shape
    last = padded - LANES
    shift = lines - last
    extra = summed[0, :, last:] + summed[1, :, last:]
    lane = iota((share, LANES), 1)
    square = jnp.sum(jnp.where(lane == shift + experts, extra, 0.0), axis=1, keepdims=True)
    inverse_rms = lax.rsqrt(square / model_width + norm_eps)
    logits = []
    for k in range(out_ref.shape[0]):
        wanted = lane == routes_ref[:, k : k + 1] + shift
        logits.append(jnp.sum(jnp.where(wanted, extra, 0.0), axis=1, keepdims=True) * inverse_rms)
    peak = functools.reduce(jnp.maximum, logits)
    shares = [jnp.exp(v - peak) for v in logits]
    total = functools.reduce(jnp.add, shares)
    inside = iota((share, padded), 1) < lines
    for k in range(out_ref.shape[0]):
        gate = summed[2 * k] * inverse_rms
        up = summed[2 * k + 1] * inverse_rms
        act = gate / (1.0 + jnp.exp(-gate)) * up
        out_ref[k] = jnp.where(inside, act * (shares[k] / total), 0.0).astype(jnp.bfloat16)


def down_kernel(me_ref, routes_ref, *refs):
    down_ref, out_ref, act_ref = refs[-3:]
    chunks = refs[:-3]
    e = pl.program_id(0)
    topk, share, _ = chunks[0].shape
    lines = down_ref.shape[2]

    @pl.when(e == 0)
    def _():
        me = me_ref[0]
        out_ref[...] = jnp.zeros_like(out_ref)
        for o, chunk in enumerate(chunks):
            begin = pl.multiple_of((me ^ o) * share, share)
            act_ref[:, pl.ds(begin, share), :] = chunk[...]

    mine = jnp.zeros((act_ref.shape[1], lines), jnp.float32)
    for k in range(topk):
        chosen = routes_ref[:, k : k + 1] == e
        mine = mine + jnp.where(chosen, act_ref[k, :, :lines].astype(jnp.float32), 0.0)
    out_ref[...] += jnp.dot(
        mine.astype(jnp.bfloat16), down_ref[0, 0], preferred_element_type=jnp.float32
    )


def experts_part(h_mid, moe_gain, w_router, expert_lines, routes):
    rows = lax.axis_size("row")
    cols = lax.axis_size("col")
    row_index = lax.axis_index("row")
    col_index = lax.axis_index("col")
    experts, _, lines, width = expert_lines.shape
    own, _ = h_mid.shape
    tokens = own * rows
    topk = routes.shape[1]
    share = tokens // cols
    padded = up_to(lines + experts + 1, LANES)
    shift = lines - (padded - LANES)
    me = col_index.astype(jnp.int32).reshape(1)

    order = row_index ^ jnp.arange(rows, dtype=jnp.int32)
    routes = routes.reshape(rows, own, topk)[order].reshape(tokens, topk)
    my_routes = lax.dynamic_slice_in_dim(routes, col_index * share, share, 0)
    router = jnp.pad(w_router, ((0, 0), (shift, LANES - shift - experts)))
    every_h = jnp.concatenate(
        [h_mid] + [from_peer(h_mid, "row", o) for o in range(1, rows)], axis=0
    )
    part_spec = lambda part: pl.BlockSpec((1, 1, lines, width), lambda e, me: (e, part, 0, 0))
    whole = lambda a: pl.BlockSpec(a.shape, lambda e, me: (0,) * a.ndim)
    gain = moe_gain.reshape(1, width)
    partial = pl.pallas_call(
        gate_up_kernel,
        grid_spec=pltpu.PrefetchScalarGridSpec(
            num_scalar_prefetch=1,
            grid=(experts,),
            in_specs=[whole(every_h), whole(gain), whole(router), whole(routes)]
            + [part_spec(0), part_spec(1)],
            out_specs=pl.BlockSpec((cols, 2 * topk, share, padded), lambda e, me: (0, 0, 0, 0)),
            scratch_shapes=[pltpu.VMEM((2 * topk, tokens, padded), jnp.float32)],
        ),
        out_shape=jax.ShapeDtypeStruct((cols, 2 * topk, share, padded), jnp.bfloat16),
        compiler_params=params(),
        cost_estimate=pl.CostEstimate(
            flops=4 * experts * tokens * lines * width,
            bytes_accessed=4 * experts * lines * width,
            transcendentals=0,
        ),
        name="gate_up",
    )(me, every_h, gain, router, routes, expert_lines, expert_lines)
    gathered = [partial[0]] + [from_peer(partial[o], "col", o) for o in range(1, cols)]
    activated = pl.pallas_call(
        functools.partial(activate_kernel, lines, experts, width * cols),
        out_shape=jax.ShapeDtypeStruct((topk, share, padded), jnp.bfloat16),
        compiler_params=params(),
        name="activate",
    )(my_routes, *gathered)
    chunks = [activated] + [from_peer(activated, "col", o) for o in range(1, cols)]
    produced = pl.pallas_call(
        down_kernel,
        grid_spec=pltpu.PrefetchScalarGridSpec(
            num_scalar_prefetch=1,
            grid=(experts,),
            in_specs=[whole(routes)] + [whole(c) for c in chunks] + [part_spec(2)],
            out_specs=pl.BlockSpec((tokens, width), lambda e, me: (0, 0)),
            scratch_shapes=[pltpu.VMEM((topk, tokens, padded), jnp.bfloat16)],
        ),
        out_shape=jax.ShapeDtypeStruct((tokens, width), jnp.float32),
        compiler_params=params(),
        cost_estimate=pl.CostEstimate(
            flops=2 * experts * tokens * lines * width,
            bytes_accessed=2 * experts * lines * width,
            transcendentals=0,
        ),
        name="down",
    )(me, routes, *chunks, expert_lines)
    blocks = produced.reshape(rows, own, width)
    mixed = blocks[0]
    for o in range(1, rows):
        mixed = mixed + from_peer(blocks[o], "row", o)
    return mixed


def local(
    hidden,
    queries,
    new_kv,
    prompt_kv,
    suffix_kv,
    lengths,
    w_out,
    moe_gain,
    w_router,
    expert_weights,
    old_lines,
    new_lines,
    routes,
):
    expert_lines = jnp.transpose(expert_weights, (0, 2, 1, 3))
    moved = migrate(expert_lines, old_lines, new_lines)
    attended = attend(queries, new_kv, prompt_kv, suffix_kv, lengths)
    projected = jnp.dot(attended, w_out, preferred_element_type=jnp.float32)
    h_mid = (hidden.astype(jnp.float32) + projected).astype(jnp.bfloat16)
    mixed = experts_part(h_mid, moe_gain, w_router, expert_lines, routes)
    return (h_mid.astype(jnp.float32) + mixed, jnp.transpose(moved, (0, 2, 1, 3)))


def solution(mesh):
    return jax.shard_map(
        local,
        mesh=mesh,
        in_specs=(
            P("row", "col"),
            P("row", None),
            P("row", None, None),
            P("row", None, "col", None),
            P("row", None, "col", None),
            P("row"),
            P(None, "col"),
            P("col"),
            P("col", None),
            P(None, "row", None, "col"),
            P(),
            P(),
            P(),
        ),
        out_specs=(P("row", "col"), P(None, "row", None, "col")),
        check_vma=False,
    )
```

time: 925 us -> 347 us (0.38)
  local copies, waits for them, and re-layouts: 634 us -> 19.7 us
  blocking collectives: 195 us -> 0 us
  waiting for transfers between devices: 29.8 us -> 152 us
  Pallas kernels: 0 us -> 119 us
  starting transfers between devices: 6.05 us -> 42.4 us
  other arithmetic: 24.9 us -> 4.18 us
  between operations: 15.3 us -> 1.09 us
  matrix products: 18.5 us -> 7.44 us
    unnamed x35 -> x37, local copies, waits for them, and re-layouts: 361 us -> 11.1 us
    all_gather x4 -> x0, blocking collectives: 169 us -> none  [the longest x1 125 us: local(): lax.all_gather(scaled, 'row', axis=0, tiled=True)]
    gather x12 -> x1, local copies, waits for them, and re-layouts: 144 us -> 0.58 us  [experts_part(): routes = routes.reshape(rows, own, topk)[order].reshape(tokens, topk)]
    pallas_call x0 -> x11, Pallas kernels: none -> 119 us  [the longest x3 47 us: unpack(): pl.pallas_call(functools.partial(unpack_kernel, rows), grid_spec=pltpu.Pr...]
    reshape x4 -> x6, local copies, waits for them, and re-layouts: 92.7 us -> 0.34 us  [the longest x3 0.21 us: experts_part(): routes = routes.reshape(rows, own, topk)[order].reshape(tokens, topk)]
    all_to_all x1 -> x3, waiting for transfers between devices: 0.01 us -> 86.3 us  [migrate(): lax.all_to_all(block, 'row', split_axis=0, concat_axis=0, tiled=True)]
    ppermute x0 -> x23, waiting for transfers between devices: none -> 65.3 us  [from_peer(): return lax.ppermute(block, axis, [(i, i ^ offset) for i in range(size)])]
    reduce_scatter x1 -> x0, waiting for transfers between devices: 29.7 us -> none  [local(): lax.psum_scatter(jnp.sum(chosen_out * gates[:, :, None], axis=1), 'row',...]
  transfers between devices with their start and end apart: 3 -> 26, of which waited for: 1 -> 12; matrix products, arithmetic and copies ran while one was open for 27% -> 6% of each run, Pallas kernels for 0% -> 24%
where the time goes in v1:
time: 347 us; the launch traced here: 346 us
  waiting for transfers between devices  152 us (44%)
  Pallas kernels  119 us (34%)
  starting transfers between devices  42.4 us (12%)
  local copies, waits for them, and re-layouts  19.7 us (6%)
  matrix products  7.44 us (2%)
  other arithmetic  4.18 us (1%)
    all_to_all x3, waiting for transfers between devices, migrate(): lax.all_to_all(block, 'row', split_axis=0, concat_axis=0, tiled=True)  86.3 us
    ppermute x23, waiting for transfers between devices, from_peer(): return lax.ppermute(block, axis, [(i, i ^ offset) for i in range(size)])  65.3 us
    pallas_call x3, Pallas kernels, unpack(): pl.pallas_call(functools.partial(unpack_kernel, rows), grid_spec=pltpu.Pr...  47 us
    pallas_call x3, Pallas kernels, pack(): pl.pallas_call(functools.partial(pack_kernel, rows), grid_spec=pltpu.Pref...  39.5 us
    ppermute x23, starting transfers between devices, from_peer(): return lax.ppermute(block, axis, [(i, i ^ offset) for i in range(size)])  27.7 us
    pallas_call x2, Pallas kernels, call_plan(): pl.pallas_call(functools.partial(kernel, lines, rows), out_shape=(stack,...  17.7 us
    all_to_all x3, starting transfers between devices, migrate(): lax.all_to_all(block, 'row', split_axis=0, concat_axis=0, tiled=True)  14.8 us
    unnamed x37, local copies, waits for them, and re-layouts  11.1 us
  transfers between devices with their start and end apart: 26, of which 12 were waited for; matrix products, arithmetic and copies ran while one was open for 6% of the time, Pallas kernels for 24%

profile of v1, /device:TPU:0, one launch (start us, length us, event | category | flops | bytes accessed | tf_op | source)
XLA Modules:
  0.0 345.7 jit_solution(1558460745587683872)
XLA Ops:
  2.4 7.9 %outgoing_plan.1 = (s32[8,1,768]{2,1,0:T(1,128)S(1)}, s32[4,64,128]{2,1,0:T(8,128)S(1)}) custom-call(s32[8,5632]{1,0:T(8,128)S(1)} %copy-done.3, s32[8,768]{1,0:T(8,128)S(1)} %pad.13.held_ref), custom_call_target="tpu_custom_call" | custom-call | flops 230686720 | bytes 360448 | tf_op jit(solution)/shard_map/outgoing_plan/pallas_call | solution.py:218
  10.5 13.2 %pack_lines.5 = bf16[8,704,512]{2,1,0:T(8,128)(2,1)S(1)} custom-call(s32[256]{0:T(256)S(1)} %reshape_squeeze.28.plan_ref, s32[8,1,768]{2,1,0:T(1,128)S(1)} %get-tuple-element.9.place_ref, bf16[8,3,704,512]{3,2,1,0:T(8,128)(2,1)} %bitcast.85), custom_call_target="tpu_custom_call" | custom-call | flops 5444206592 | bytes 11534336 | tf_op jit(solution)/shard_map/pack_lines/pallas_call | solution.py:234
  23.7 2.5 copy-done.2
  26.2 5.2 %all-to-all-start.2 = ((bf16[8,704,512]{2,1,0:T(8,128)(2,1)}), bf16[8,704,512]{2,1,0:T(8,128)(2,1)}, u32[]{:S(2)}, u32[]{:S(2)}) async-start(bf16[8,704,512]{2,1,0:T(8,128)(2,1)} %copy-done.2), calls=%async_computation.2 | async-start | bytes 11534336 | tf_op jit(solution)/shard_map/all_to_all | solution.py:315
  31.4 13.2 %pack_lines.4 = bf16[8,704,512]{2,1,0:T(8,128)(2,1)S(1)} custom-call(s32[256]{0:T(256)S(1)} %reshape_squeeze.28.plan_ref, s32[8,1,768]{2,1,0:T(1,128)S(1)} %get-tuple-element.9.place_ref, bf16[8,3,704,512]{3,2,1,0:T(8,128)(2,1)} %bitcast.86), custom_call_target="tpu_custom_call" | custom-call | flops 5444206592 | bytes 11534336 | tf_op jit(solution)/shard_map/pack_lines/pallas_call | solution.py:234
  44.6 2.5 copy-done.1
  47.1 50.5 %all-to-all-done.2.block_ref = bf16[8,704,512]{2,1,0:T(8,128)(2,1)} async-done(((bf16[8,704,512]{2,1,0:T(8,128)(2,1)}), bf16[8,704,512]{2,1,0:T(8,128)(2,1)}, u32[]{:S(2)}, u32[]{:S(2)}) %all-to-all-start.2) | async-done | bytes 5767200 | tf_op jit(solution)/shard_map/all_to_all | solution.py:315
  97.6 4.7 %all-to-all-start.1 = ((bf16[8,704,512]{2,1,0:T(8,128)(2,1)}), bf16[8,704,512]{2,1,0:T(8,128)(2,1)}, u32[]{:S(2)}, u32[]{:S(2)}) async-start(bf16[8,704,512]{2,1,0:T(8,128)(2,1)} %copy-done.1), calls=%async_computation.1 | async-start | bytes 11534336 | tf_op jit(solution)/shard_map/all_to_all | solution.py:315
  105.9 2.7 fusion.35
  116.8 13.2 %pack_lines.3 = bf16[8,704,512]{2,1,0:T(8,128)(2,1)S(1)} custom-call(s32[256]{0:T(256)S(1)} %reshape_squeeze.28.plan_ref, s32[8,1,768]{2,1,0:T(1,128)S(1)} %get-tuple-element.9.place_ref, bf16[8,3,704,512]{3,2,1,0:T(8,128)(2,1)} %bitcast.87), custom_call_target="tpu_custom_call" | custom-call | flops 5444206592 | bytes 11534336 | tf_op jit(solution)/shard_map/pack_lines/pallas_call | solution.py:234
  130.0 2.5 copy-done
  132.5 35.8 %all-to-all-done.1.block_ref = bf16[8,704,512]{2,1,0:T(8,128)(2,1)} async-done(((bf16[8,704,512]{2,1,0:T(8,128)(2,1)}), bf16[8,704,512]{2,1,0:T(8,128)(2,1)}, u32[]{:S(2)}, u32[]{:S(2)}) %all-to-all-start.1) | async-done | bytes 5767200 | tf_op jit(solution)/shard_map/all_to_all | solution.py:315
  168.3 4.9 %all-to-all-start = ((bf16[8,704,512]{2,1,0:T(8,128)(2,1)}), bf16[8,704,512]{2,1,0:T(8,128)(2,1)}, u32[]{:S(2)}, u32[]{:S(2)}) async-start(bf16[8,704,512]{2,1,0:T(8,128)(2,1)} %copy-done), calls=%async_computation | async-start | bytes 11534336 | tf_op jit(solution)/shard_map/all_to_all | solution.py:315
  174.5 2.4 collective-permute-start
  176.9 2.6 collective-permute-start.1
  179.5 3.4 collective-permute-done
  182.9 7.2 %collective-permute-done.1 = f32[8,4224]{1,0:T(8,128)S(1)} collective-permute-done((f32[8,4224]{1,0:T(8,128)S(1)}, f32[8,4224]{1,0:T(8,128)S(1)}, u32[]{:S(2)}, u32[]{:S(2)}) %collective-permute-start.1) | collective-permute-done | bytes 135200 | tf_op jit(solution)/shard_map/ppermute | solution.py:325
  190.6 2.9 constant_dynamic-update-slice_fusion.7
  194.6 1.8 collective-permute-start.4
  198.2 2.6 collective-permute-start.8
  200.8 37.5 %collective-permute-done.4 = bf16[8,512]{1,0:T(8,128)(2,1)S(1)} collective-permute-done((bf16[8,512]{1,0:T(8,128)(2,1)S(1)}, bf16[8,512]{1,0:T(8,128)(2,1)S(1)}, u32[]{:S(2)}, u32[]{:S(2)}) %collective-permute-start.4) | collective-permute-done | bytes 8224 | tf_op jit(solution)/shard_map/ppermute | solution.py:325
  239.4 2.9 collective-permute-done.9
  242.3 8.7 %gate_up.1 = bf16[4,4,16,768]{3,2,1,0:T(8,128)(2,1)S(1)} custom-call(s32[1]{0:T(128)} %bitcast.19.me_ref, bf16[64,512]{1,0:T(8,128)(2,1)S(1)} %constant_dynamic-update-slice_fusion.h_ref, bf16[1,512]{1,0:T(2,128)(2,1)S(1)} %reshape.114.gain_ref, bf16[512,128]{1,0:T(8,128)(2,1)S(1)} %pad.11.router_ref, s32[64,2]{1,0:T(8,128)S(1)} %bitcast.82, ...), custom_call_target="tpu_custom_call" | custom-call | flops 738197504 | bytes 11534336 | tf_op jit(solution)/shard_map/gate_up/pallas_call | solution.py:515
  251.1 2.4 collective-permute-start.10
  253.5 2.6 collective-permute-start.11
  256.1 7.6 %collective-permute-done.11.refs_2_ = bf16[4,16,768]{2,1,0:T(8,128)(2,1)S(1)} collective-permute-done((bf16[4,16,768]{2,1,0:T(8,128)(2,1)S(1)}, bf16[4,16,768]{2,1,0:T(8,128)(2,1)S(1)}, u32[]{:S(2)}, u32[]{:S(2)}) %collective-permute-start.11) | collective-permute-done | bytes 98336 | tf_op jit(solution)/shard_map/ppermute | solution.py:325
  269.1 1.9 collective-permute-done.14.refs_2_
  272.8 6.1 %down.1 = f32[64,512]{1,0:T(8,128)S(1)} custom-call(s32[1]{0:T(128)} %bitcast.19.me_ref, s32[64,2]{1,0:T(8,128)S(1)} %bitcast.84, bf16[2,16,768]{2,1,0:T(8,128)(2,1)S(1)} %activate.1.refs_0_, bf16[2,16,768]{2,1,0:T(8,128)(2,1)S(1)} %collective-permute-done.13.refs_1_, bf16[2,16,768]{2,1,0:T(8,128)(2,1)S(1)} %collective-permute-done.14.refs_2_, ...), custom_call_target="tpu_custom_call" | custom-call | flops 369098752 | bytes 5767168 | tf_op jit(solution)/shard_map/down/pallas_call | solution.py:542
  280.1 9.8 %incoming_plan.1 = (f32[768,128]{1,0:T(8,128)S(1)}, s32[4,64,128]{2,1,0:T(8,128)S(1)}) custom-call(s32[8,5632]{1,0:T(8,128)S(1)} %copy-done.4, s32[8,768]{1,0:T(8,128)S(1)} %pad.12.wanted_ref), custom_call_target="tpu_custom_call" | custom-call | flops 230686720 | bytes 360448 | tf_op jit(solution)/shard_map/incoming_plan/pallas_call | solution.py:218
  298.7 15.7 %unpack_lines.3.rest_0_ = bf16[8,3,704,512]{3,2,1,0:T(8,128)(2,1)} custom-call(s32[256]{0:T(256)S(1)} %reshape_squeeze.27.plan_ref, f32[768,128]{1,0:T(8,128)S(1)} %get-tuple-element.7.place_ref, bf16[8,704,512]{2,1,0:T(8,128)(2,1)} %all-to-all-done.2.block_ref), custom_call_target="tpu_custom_call" | custom-call | flops 5905580032 | bytes 11534336 | tf_op jit(solution)/shard_map/unpack_lines/pallas_call | solution.py:270
  314.4 15.7 %unpack_lines.4.rest_0_ = bf16[8,3,704,512]{3,2,1,0:T(8,128)(2,1)} custom-call(s32[256]{0:T(256)S(1)} %reshape_squeeze.27.plan_ref, f32[768,128]{1,0:T(8,128)S(1)} %get-tuple-element.7.place_ref, bf16[8,704,512]{2,1,0:T(8,128)(2,1)} %all-to-all-done.1.block_ref, bf16[8,3,704,512]{3,2,1,0:T(8,128)(2,1)} %unpack_lines.3.rest_0_), custom_call_target="tpu_custom_call", output_to_operand_aliasing={{}: (3, {})} | custom-call | flops 5905580032 | bytes 11534336 | tf_op jit(solution)/shard_map/unpack_lines/pallas_call | solution.py:270
  330.0 15.7 %unpack_lines.5 = bf16[8,3,704,512]{3,2,1,0:T(8,128)(2,1)} custom-call(s32[256]{0:T(256)S(1)} %reshape_squeeze.27.plan_ref, f32[768,128]{1,0:T(8,128)S(1)} %get-tuple-element.7.place_ref, bf16[8,704,512]{2,1,0:T(8,128)(2,1)} %all-to-all-done.block_ref, bf16[8,3,704,512]{3,2,1,0:T(8,128)(2,1)} %unpack_lines.4.rest_0_), custom_call_target="tpu_custom_call", output_to_operand_aliasing={{}: (3, {})} | custom-call | flops 5905580032 | bytes 11534336 | tf_op jit(solution)/shard_map/unpack_lines/pallas_call | solution.py:270
  (120 shorter events, 36.6 us)
Async XLA Ops:
  26.2 71.4 %all-to-all-start.2 = ((bf16[8,704,512]{2,1,0:T(8,128)(2,1)}), bf16[8,704,512]{2,1,0:T(8,128)(2,1)}, u32[]{:S(2)}, u32[]{:S(2)}) async-start(bf16[8,704,512]{2,1,0:T(8,128)(2,1)} %copy-done.2), calls=%async_computation.2 | async-start | bytes 11534336 | tf_op jit(solution)/shard_map/all_to_all | solution.py:315
  97.6 70.7 %all-to-all-start.1 = ((bf16[8,704,512]{2,1,0:T(8,128)(2,1)}), bf16[8,704,512]{2,1,0:T(8,128)(2,1)}, u32[]{:S(2)}, u32[]{:S(2)}) async-start(bf16[8,704,512]{2,1,0:T(8,128)(2,1)} %copy-done.1), calls=%async_computation.1 | async-start | bytes 11534336 | tf_op jit(solution)/shard_map/all_to_all | solution.py:315
  132.5 40.9 %copy-start.7 = (bf16[8,16,2]{0,2,1:T(2,128)(2,1)S(1)}, bf16[8,16,2]{0,2,1:T(2,128)(2,1)}, u32[]{:S(2)}) copy-start(bf16[8,16,2]{0,2,1:T(2,128)(2,1)} %get-tuple-element.12) | copy-start | bytes 1540
  168.3 161.8 %all-to-all-start = ((bf16[8,704,512]{2,1,0:T(8,128)(2,1)}), bf16[8,704,512]{2,1,0:T(8,128)(2,1)}, u32[]{:S(2)}, u32[]{:S(2)}) async-start(bf16[8,704,512]{2,1,0:T(8,128)(2,1)} %copy-done), calls=%async_computation | async-start | bytes 11534336 | tf_op jit(solution)/shard_map/all_to_all | solution.py:315
  173.2 17.4 %copy-start.8 = (bf16[8,512]{1,0:T(8,128)(2,1)S(1)}, bf16[8,512]{1,0:T(8,128)(2,1)}, u32[]{:S(2)}) copy-start(bf16[8,512]{1,0:T(8,128)(2,1)} %param.13) | copy-start | bytes 24580
  173.3 20.1 %copy-start.10 = (s32[64,2]{0,1:T(2,128)S(1)}, s32[64,2]{0,1:T(2,128)}, u32[]{:S(2)}) copy-start(s32[64,2]{0,1:T(2,128)} %param.25) | copy-start | bytes 1540
  173.3 20.9 %copy-start.9 = (bf16[512,8]{0,1:T(8,128)(2,1)S(1)}, bf16[512,8]{0,1:T(8,128)(2,1)}, u32[]{:S(2)}) copy-start(bf16[512,8]{0,1:T(8,128)(2,1)} %param.21) | copy-start | bytes 24580
  173.4 21.1 %copy-start.11 = (bf16[512]{0:T(512)(128)(2,1)S(1)}, bf16[512]{0:T(512)(128)(2,1)}, u32[]{:S(2)}) copy-start(bf16[512]{0:T(512)(128)(2,1)} %param.20) | copy-start | bytes 3076
  174.5 8.3 %collective-permute-start = (f32[8,4224]{1,0:T(8,128)S(1)}, f32[8,4224]{1,0:T(8,128)S(1)}, u32[]{:S(2)}, u32[]{:S(2)}) collective-permute-start(f32[8,4224]{1,0:T(8,128)S(1)} %concatenate.6), channel_id=1, source_target_pairs={{0,1},{1,0},{2,3},{3,2},{4,5},{5,4},{6,7},{7,6},{8,9},{9,8},{10,11... | collective-permute-start | bytes 405512 | tf_op jit(solution)/shard_map/ppermute | solution.py:325
  176.9 13.2 %collective-permute-start.1 = (f32[8,4224]{1,0:T(8,128)S(1)}, f32[8,4224]{1,0:T(8,128)S(1)}, u32[]{:S(2)}, u32[]{:S(2)}) collective-permute-start(f32[8,4224]{1,0:T(8,128)S(1)} %concatenate.6), channel_id=1, source_target_pairs={{0,2},{1,3},{2,0},{3,1},{4,6},{5,7},{6,4},{7,5},{8,10},{9,11},{10,... | collective-permute-start | bytes 405512 | tf_op jit(solution)/shard_map/ppermute | solution.py:325
  179.5 10.6 %collective-permute-start.2 = (f32[8,4224]{1,0:T(8,128)S(1)}, f32[8,4224]{1,0:T(8,128)S(1)}, u32[]{:S(2)}, u32[]{:S(2)}) collective-permute-start(f32[8,4224]{1,0:T(8,128)S(1)} %concatenate.6), channel_id=1, source_target_pairs={{0,3},{1,2},{2,1},{3,0},{4,7},{5,6},{6,5},{7,4},{8,11},{9,10},{10,... | collective-permute-start | bytes 405512 | tf_op jit(solution)/shard_map/ppermute | solution.py:325
  193.4 4.8 %collective-permute-start.3 = (bf16[8,512]{1,0:T(8,128)(2,1)S(1)}, bf16[8,512]{1,0:T(8,128)(2,1)S(1)}, u32[]{:S(2)}, u32[]{:S(2)}) collective-permute-start(bf16[8,512]{1,0:T(8,128)(2,1)S(1)} %get-tuple-element.36), channel_id=1, source_target_pairs={{0,4},{4,0},{8,12},{12,8},{16,20},{20,16},{24,28},{28,24},{1,5},{5... | collective-permute-start | bytes 24584 | tf_op jit(solution)/shard_map/ppermute | solution.py:325
  194.6 43.7 %collective-permute-start.4 = (bf16[8,512]{1,0:T(8,128)(2,1)S(1)}, bf16[8,512]{1,0:T(8,128)(2,1)S(1)}, u32[]{:S(2)}, u32[]{:S(2)}) collective-permute-start(bf16[8,512]{1,0:T(8,128)(2,1)S(1)} %get-tuple-element.36), channel_id=1, source_target_pairs={{0,8},{4,12},{8,0},{12,4},{16,24},{20,28},{24,16},{28,20},{1,9},{5... | collective-permute-start | bytes 24584 | tf_op jit(solution)/shard_map/ppermute | solution.py:325
  196.3 42.7 %collective-permute-start.5 = (bf16[8,512]{1,0:T(8,128)(2,1)S(1)}, bf16[8,512]{1,0:T(8,128)(2,1)S(1)}, u32[]{:S(2)}, u32[]{:S(2)}) collective-permute-start(bf16[8,512]{1,0:T(8,128)(2,1)S(1)} %get-tuple-element.36), channel_id=1, source_target_pairs={{0,12},{4,8},{8,4},{12,0},{16,28},{20,24},{24,20},{28,16},{1,13},{... | collective-permute-start | bytes 24584 | tf_op jit(solution)/shard_map/ppermute | solution.py:325
  196.5 42.5 %collective-permute-start.6 = (bf16[8,512]{1,0:T(8,128)(2,1)S(1)}, bf16[8,512]{1,0:T(8,128)(2,1)S(1)}, u32[]{:S(2)}, u32[]{:S(2)}) collective-permute-start(bf16[8,512]{1,0:T(8,128)(2,1)S(1)} %get-tuple-element.36), channel_id=1, source_target_pairs={{0,16},{4,20},{8,24},{12,28},{16,0},{20,4},{24,8},{28,12},{1,17},{... | collective-permute-start | bytes 24584 | tf_op jit(solution)/shard_map/ppermute | solution.py:325
  198.2 40.8 %collective-permute-start.7 = (bf16[8,512]{1,0:T(8,128)(2,1)S(1)}, bf16[8,512]{1,0:T(8,128)(2,1)S(1)}, u32[]{:S(2)}, u32[]{:S(2)}) collective-permute-start(bf16[8,512]{1,0:T(8,128)(2,1)S(1)} %get-tuple-element.36), channel_id=1, source_target_pairs={{0,20},{4,16},{8,28},{12,24},{16,4},{20,0},{24,12},{28,8},{1,21},{... | collective-permute-start | bytes 24584 | tf_op jit(solution)/shard_map/ppermute | solution.py:325
  198.2 41.2 %collective-permute-start.8 = (bf16[8,512]{1,0:T(8,128)(2,1)S(1)}, bf16[8,512]{1,0:T(8,128)(2,1)S(1)}, u32[]{:S(2)}, u32[]{:S(2)}) collective-permute-start(bf16[8,512]{1,0:T(8,128)(2,1)S(1)} %get-tuple-element.36), channel_id=1, source_target_pairs={{0,24},{4,28},{8,16},{12,20},{16,8},{20,12},{24,0},{28,4},{1,25},{... | collective-permute-start | bytes 24584 | tf_op jit(solution)/shard_map/ppermute | solution.py:325
  238.3 4.0 %collective-permute-start.9 = (bf16[8,512]{1,0:T(8,128)(2,1)S(1)}, bf16[8,512]{1,0:T(8,128)(2,1)S(1)}, u32[]{:S(2)}, u32[]{:S(2)}) collective-permute-start(bf16[8,512]{1,0:T(8,128)(2,1)S(1)} %get-tuple-element.36), channel_id=1, source_target_pairs={{0,28},{4,24},{8,20},{12,16},{16,12},{20,8},{24,4},{28,0},{1,29},{... | collective-permute-start | bytes 24584 | tf_op jit(solution)/shard_map/ppermute | solution.py:325
  251.1 5.0 %collective-permute-start.10 = (bf16[4,16,768]{2,1,0:T(8,128)(2,1)S(1)}, bf16[4,16,768]{2,1,0:T(8,128)(2,1)S(1)}, u32[]{:S(2)}, u32[]{:S(2)}) collective-permute-start(bf16[4,16,768]{2,1,0:T(8,128)(2,1)S(1)} %get-tuple-element.20), channel_id=1, source_target_pairs={{0,1},{1,0},{2,3},{3,2},{4,5},{5,4},{6,7},{7,6},{8,9},{9,8},{10,11... | collective-permute-start | bytes 294920 | tf_op jit(solution)/shard_map/ppermute | solution.py:325
  253.5 10.2 %collective-permute-start.11 = (bf16[4,16,768]{2,1,0:T(8,128)(2,1)S(1)}, bf16[4,16,768]{2,1,0:T(8,128)(2,1)S(1)}, u32[]{:S(2)}, u32[]{:S(2)}) collective-permute-start(bf16[4,16,768]{2,1,0:T(8,128)(2,1)S(1)} %get-tuple-element.19), channel_id=1, source_target_pairs={{0,2},{1,3},{2,0},{3,1},{4,6},{5,7},{6,4},{7,5},{8,10},{9,11},{10,... | collective-permute-start | bytes 294920 | tf_op jit(solution)/shard_map/ppermute | solution.py:325
  256.1 7.6 %collective-permute-start.12 = (bf16[4,16,768]{2,1,0:T(8,128)(2,1)S(1)}, bf16[4,16,768]{2,1,0:T(8,128)(2,1)S(1)}, u32[]{:S(2)}, u32[]{:S(2)}) collective-permute-start(bf16[4,16,768]{2,1,0:T(8,128)(2,1)S(1)} %get-tuple-element.18), channel_id=1, source_target_pairs={{0,3},{1,2},{2,1},{3,0},{4,7},{5,6},{6,5},{7,4},{8,11},{9,10},{10,... | collective-permute-start | bytes 294920 | tf_op jit(solution)/shard_map/ppermute | solution.py:325
  263.8 5.3 %collective-permute-start.13 = (bf16[2,16,768]{2,1,0:T(8,128)(2,1)S(1)}, bf16[2,16,768]{2,1,0:T(8,128)(2,1)S(1)}, u32[]{:S(2)}, u32[]{:S(2)}) collective-permute-start(bf16[2,16,768]{2,1,0:T(8,128)(2,1)S(1)} %activate.1.refs_0_), channel_id=1, source_target_pairs={{0,1},{1,0},{2,3},{3,2},{4,5},{5,4},{6,7},{7,6},{8,9},{9,8},{10,11... | collective-permute-start | bytes 147464 | tf_op jit(solution)/shard_map/ppermute | solution.py:325
  265.5 5.6 %collective-permute-start.14 = (bf16[2,16,768]{2,1,0:T(8,128)(2,1)S(1)}, bf16[2,16,768]{2,1,0:T(8,128)(2,1)S(1)}, u32[]{:S(2)}, u32[]{:S(2)}) collective-permute-start(bf16[2,16,768]{2,1,0:T(8,128)(2,1)S(1)} %activate.1.refs_0_), channel_id=1, source_target_pairs={{0,2},{1,3},{2,0},{3,1},{4,6},{5,7},{6,4},{7,5},{8,10},{9,11},{10,... | collective-permute-start | bytes 147464 | tf_op jit(solution)/shard_map/ppermute | solution.py:325
  266.9 5.9 %collective-permute-start.15 = (bf16[2,16,768]{2,1,0:T(8,128)(2,1)S(1)}, bf16[2,16,768]{2,1,0:T(8,128)(2,1)S(1)}, u32[]{:S(2)}, u32[]{:S(2)}) collective-permute-start(bf16[2,16,768]{2,1,0:T(8,128)(2,1)S(1)} %activate.1.refs_0_), channel_id=1, source_target_pairs={{0,3},{1,2},{2,1},{3,0},{4,7},{5,6},{6,5},{7,4},{8,11},{9,10},{10,... | collective-permute-start | bytes 147464 | tf_op jit(solution)/shard_map/ppermute | solution.py:325
  269.1 11.0 %copy-start.4 = (s32[8,5632]{1,0:T(8,128)S(1)}, s32[8,5632]{1,0:T(8,128)}, u32[]{:S(2)}) copy-start(s32[8,5632]{1,0:T(8,128)} %old_ref.1) | copy-start | bytes 540676
  279.0 13.5 %collective-permute-start.16 = (f32[8,512]{1,0:T(8,128)S(1)}, f32[8,512]{1,0:T(8,128)S(1)}, u32[]{:S(2)}, u32[]{:S(2)}) collective-permute-start(f32[8,512]{1,0:T(8,128)S(1)} %get-tuple-element.22), channel_id=1, source_target_pairs={{0,4},{4,0},{8,12},{12,8},{16,20},{20,16},{24,28},{28,24},{1,5},{5... | collective-permute-start | bytes 49160 | tf_op jit(solution)/shard_map/ppermute | solution.py:325
  279.1 15.0 %collective-permute-start.17 = (f32[8,512]{1,0:T(8,128)S(1)}, f32[8,512]{1,0:T(8,128)S(1)}, u32[]{:S(2)}, u32[]{:S(2)}) collective-permute-start(f32[8,512]{1,0:T(8,128)S(1)} %get-tuple-element.28), channel_id=1, source_target_pairs={{0,8},{4,12},{8,0},{12,4},{16,24},{20,28},{24,16},{28,20},{1,9},{5... | collective-permute-start | bytes 49160 | tf_op jit(solution)/shard_map/ppermute | solution.py:325
  290.0 5.5 %collective-permute-start.18 = (f32[8,512]{1,0:T(8,128)S(1)}, f32[8,512]{1,0:T(8,128)S(1)}, u32[]{:S(2)}, u32[]{:S(2)}) collective-permute-start(f32[8,512]{1,0:T(8,128)S(1)} %get-tuple-element.27), channel_id=1, source_target_pairs={{0,12},{4,8},{8,4},{12,0},{16,28},{20,24},{24,20},{28,16},{1,13},{... | collective-permute-start | bytes 49160 | tf_op jit(solution)/shard_map/ppermute | solution.py:325
  290.8 4.6 %collective-permute-start.19 = (f32[8,512]{1,0:T(8,128)S(1)}, f32[8,512]{1,0:T(8,128)S(1)}, u32[]{:S(2)}, u32[]{:S(2)}) collective-permute-start(f32[8,512]{1,0:T(8,128)S(1)} %get-tuple-element.26), channel_id=1, source_target_pairs={{0,16},{4,20},{8,24},{12,28},{16,0},{20,4},{24,8},{28,12},{1,17},{... | collective-permute-start | bytes 49160 | tf_op jit(solution)/shard_map/ppermute | solution.py:325
  292.3 3.2 collective-permute-start.20
  292.5 4.6 %collective-permute-start.21 = (f32[8,512]{1,0:T(8,128)S(1)}, f32[8,512]{1,0:T(8,128)S(1)}, u32[]{:S(2)}, u32[]{:S(2)}) collective-permute-start(f32[8,512]{1,0:T(8,128)S(1)} %get-tuple-element.24), channel_id=1, source_target_pairs={{0,24},{4,28},{8,16},{12,20},{16,8},{20,12},{24,0},{28,4},{1,25},{... | collective-permute-start | bytes 49160 | tf_op jit(solution)/shard_map/ppermute | solution.py:325
  294.0 4.1 %collective-permute-start.22 = (f32[8,512]{1,0:T(8,128)S(1)}, f32[8,512]{1,0:T(8,128)S(1)}, u32[]{:S(2)}, u32[]{:S(2)}) collective-permute-start(f32[8,512]{1,0:T(8,128)S(1)} %get-tuple-element.23), channel_id=1, source_target_pairs={{0,28},{4,24},{8,20},{12,16},{16,12},{20,8},{24,4},{28,0},{1,29},{... | collective-permute-start | bytes 49160 | tf_op jit(solution)/shard_map/ppermute | solution.py:325
  (7 other events, 18.6 us)

commit v2 on v1

--- a/solution.py
+++ b/solution.py
@@ -288,41 +288,70 @@
     )(*operands)
 
 
+def after_kernel(*refs):
+    del refs
+
+
+def after(values, signals):
+    anywhere = pl.BlockSpec(memory_space=pl.ANY)
+    return pl.pallas_call(
+        after_kernel,
+        in_specs=[anywhere] * (len(values) + len(signals)),
+        out_specs=[anywhere] * len(values),
+        out_shape=[jax.ShapeDtypeStruct(v.shape, v.dtype) for v in values],
+        input_output_aliases={n: n for n in range(len(values))},
+        name="after",
+    )(*values, *signals)
+
+
 def own_ids(table, lines, width):
     mine = lax.dynamic_slice_in_dim(table, lax.axis_index("row") * lines, lines, 1)
     return jnp.pad(mine, ((0, 0), (0, width - lines)), constant_values=-1)
 
 
-def migrate(expert_lines, old_lines, new_lines):
-    rows = lax.axis_size("row")
-    experts, parts, lines, width = expert_lines.shape
-    padded = up_to(lines, LANES)
-    block_rows = up_to(experts * lines // rows, TILE)
-    deep = up_to(lines + 2 * (TILE - 1) * rows, TILE)
-    out_place, out_plan = call_plan(
-        outgoing_kernel, "outgoing_plan", new_lines, own_ids(old_lines, lines, padded),
-        lines, rows, False,
-    )
-    in_place, in_plan = call_plan(
-        incoming_kernel, "incoming_plan", old_lines, own_ids(new_lines, lines, padded),
-        lines, rows, True,
-    )
-    moved = None
-    packed = [
-        pack(expert_lines, out_place, out_plan, part, rows, block_rows, deep)
-        for part in range(parts)
-    ]
-    arrived = [lax.all_to_all(block, "row", split_axis=0, concat_axis=0, tiled=True) for block in packed]
-    for part in range(parts):
-        moved = unpack(
-            arrived[part], in_place, in_plan, part, expert_lines.shape, up_to(deep, LANES), moved
-        )
-    return moved
-
-
 def from_peer(block, axis, offset):
     size = lax.axis_size(axis)
     return lax.ppermute(block, axis, [(i, i ^ offset) for i in range(size)])
+
+
+class Migration:
+    def __init__(self, expert_lines, old_lines, new_lines):
+        rows = lax.axis_size("row")
+        experts, self.parts, lines, _ = expert_lines.shape
+        padded = up_to(lines, LANES)
+        block_rows = up_to(experts * lines // rows, TILE)
+        self.deep = up_to(lines + 2 * (TILE - 1) * rows, TILE)
+        self.shape = expert_lines.shape
+        out_place, out_plan = call_plan(
+            outgoing_kernel, "outgoing_plan", new_lines, own_ids(old_lines, lines, padded),
+            lines, rows, False,
+        )
+        self.in_place, self.in_plan = call_plan(
+            incoming_kernel, "incoming_plan", old_lines, own_ids(new_lines, lines, padded),
+            lines, rows, True,
+        )
+        self.packed = [
+            pack(expert_lines, out_place, out_plan, part, rows, block_rows, self.deep)
+            for part in range(self.parts)
+        ]
+        self.arrived = []
+
+    def send(self, part, signals=()):
+        block = self.packed[part]
+        if signals:
+            (block,) = after([block], signals)
+        self.arrived.append(
+            lax.all_to_all(block, "row", split_axis=0, concat_axis=0, tiled=True)
+        )
+
+    def finish(self):
+        moved = None
+        for part in range(self.parts):
+            moved = unpack(
+                self.arrived[part], self.in_place, self.in_plan, part, self.shape,
+                up_to(self.deep, LANES), moved,
+            )
+        return moved
 
 
 def attend(queries, new_kv, prompt_kv, suffix_kv, lengths):
@@ -488,7 +517,7 @@
     )
 
 
-def experts_part(h_mid, moe_gain, w_router, expert_lines, routes):
+def experts_part(h_mid, moe_gain, w_router, expert_lines, routes, migration):
     rows = lax.axis_size("row")
     cols = lax.axis_size("col")
     row_index = lax.axis_index("row")
@@ -509,6 +538,7 @@
     every_h = jnp.concatenate(
         [h_mid] + [from_peer(h_mid, "row", o) for o in range(1, rows)], axis=0
     )
+    migration.send(1, [every_h])
     part_spec = lambda part: pl.BlockSpec((1, 1, lines, width), lambda e, me: (e, part, 0, 0))
     whole = lambda a: pl.BlockSpec(a.shape, lambda e, me: (0,) * a.ndim)
     gain = moe_gain.reshape(1, width)
@@ -580,11 +610,14 @@
     routes,
 ):
     expert_lines = jnp.transpose(expert_weights, (0, 2, 1, 3))
-    moved = migrate(expert_lines, old_lines, new_lines)
+    migration = Migration(expert_lines, old_lines, new_lines)
+    migration.send(0)
     attended = attend(queries, new_kv, prompt_kv, suffix_kv, lengths)
     projected = jnp.dot(attended, w_out, preferred_element_type=jnp.float32)
     h_mid = (hidden.astype(jnp.float32) + projected).astype(jnp.bfloat16)
-    mixed = experts_part(h_mid, moe_gain, w_router, expert_lines, routes)
+    mixed = experts_part(h_mid, moe_gain, w_router, expert_lines, routes, migration)
+    migration.send(2, [mixed])
+    moved = migration.finish()
     return (h_mid.astype(jnp.float32) + mixed, jnp.transpose(moved, (0, 2, 1, 3)))
 
 

time: 347 us -> 277 us (0.80)
  waiting for transfers between devices: 152 us -> 79.3 us
    all_to_all x3, waiting for transfers between devices: 86.3 us -> 23.7 us  [send(): lax.all_to_all(block, 'row', split_axis=0, concat_axis=0, tiled=True)]
    ppermute x23, waiting for transfers between devices: 65.3 us -> 55.6 us  [from_peer(): return lax.ppermute(block, axis, [(i, i ^ offset) for i in range(size)])]
    unnamed x37 -> x39, local copies, waits for them, and re-layouts: 11.1 us -> 11.7 us
  transfers between devices with their start and end apart: 26 -> 26, of which waited for: 12 -> 12; matrix products, arithmetic and copies ran while one was open for 6% -> 8% of each run, Pallas kernels for 24% -> 30%
where the time goes in v2:
time: 277 us; the launch traced here: 276 us
  Pallas kernels  119 us (43%)
  waiting for transfers between devices  79.3 us (29%)
  starting transfers between devices  43.2 us (16%)
  local copies, waits for them, and re-layouts  20.3 us (7%)
  matrix products  8.15 us (3%)
  other arithmetic  4.18 us (2%)
    ppermute x23, waiting for transfers between devices, from_peer(): return lax.ppermute(block, axis, [(i, i ^ offset) for i in range(size)])  55.6 us
    pallas_call x3, Pallas kernels, unpack(): pl.pallas_call(functools.partial(unpack_kernel, rows), grid_spec=pltpu.Pr...  47 us
    pallas_call x3, Pallas kernels, pack(): pl.pallas_call(functools.partial(pack_kernel, rows), grid_spec=pltpu.Pref...  39.5 us
    ppermute x23, starting transfers between devices, from_peer(): return lax.ppermute(block, axis, [(i, i ^ offset) for i in range(size)])  28.2 us
    all_to_all x3, waiting for transfers between devices, send(): lax.all_to_all(block, 'row', split_axis=0, concat_axis=0, tiled=True)  23.7 us
    pallas_call x2, Pallas kernels, call_plan(): pl.pallas_call(functools.partial(kernel, lines, rows), out_shape=(stack,...  17.7 us
    all_to_all x3, starting transfers between devices, send(): lax.all_to_all(block, 'row', split_axis=0, concat_axis=0, tiled=True)  15.1 us
    unnamed x39, local copies, waits for them, and re-layouts  11.7 us
  transfers between devices with their start and end apart: 26, of which 12 were waited for; matrix products, arithmetic and copies ran while one was open for 8% of the time, Pallas kernels for 30%

profile of v2, /device:TPU:0, one launch (start us, length us, event | category | flops | bytes accessed | tf_op | source)
XLA Modules:
  0.0 275.6 jit_solution(9235567889173914369)
XLA Ops:
  2.4 7.9 %outgoing_plan.1 = (s32[8,1,768]{2,1,0:T(1,128)S(1)}, s32[4,64,128]{2,1,0:T(8,128)S(1)}) custom-call(s32[8,5632]{1,0:T(8,128)S(1)} %copy-done.5, s32[8,768]{1,0:T(8,128)S(1)} %pad.13.held_ref), custom_call_target="tpu_custom_call" | custom-call | flops 230686720 | bytes 360448 | tf_op jit(solution)/shard_map/outgoing_plan/pallas_call | solution.py:218
  10.5 13.2 %pack_lines.5 = bf16[8,704,512]{2,1,0:T(8,128)(2,1)S(1)} custom-call(s32[256]{0:T(256)S(1)} %reshape_squeeze.28.plan_ref, s32[8,1,768]{2,1,0:T(1,128)S(1)} %get-tuple-element.9.place_ref, bf16[8,3,704,512]{3,2,1,0:T(8,128)(2,1)} %bitcast.85), custom_call_target="tpu_custom_call" | custom-call | flops 5444206592 | bytes 11534336 | tf_op jit(solution)/shard_map/pack_lines/pallas_call | solution.py:234
  23.7 2.5 copy-done.2
  26.2 5.2 %all-to-all-start.2 = ((bf16[8,704,512]{2,1,0:T(8,128)(2,1)}), bf16[8,704,512]{2,1,0:T(8,128)(2,1)}, u32[]{:S(2)}, u32[]{:S(2)}) async-start(bf16[8,704,512]{2,1,0:T(8,128)(2,1)} %copy-done.2), calls=%async_computation.2 | async-start | bytes 11534336 | tf_op jit(solution)/shard_map/all_to_all | solution.py:344
  33.4 2.7 fusion.35
  47.9 2.6 collective-permute-start
  50.4 2.6 collective-permute-start.1
  53.0 3.7 %collective-permute-done = f32[8,4224]{1,0:T(8,128)S(1)} collective-permute-done((f32[8,4224]{1,0:T(8,128)S(1)}, f32[8,4224]{1,0:T(8,128)S(1)}, u32[]{:S(2)}, u32[]{:S(2)}) %collective-permute-start) | collective-permute-done | bytes 135200 | tf_op jit(solution)/shard_map/ppermute | solution.py:314
  56.7 6.9 %collective-permute-done.1 = f32[8,4224]{1,0:T(8,128)S(1)} collective-permute-done((f32[8,4224]{1,0:T(8,128)S(1)}, f32[8,4224]{1,0:T(8,128)S(1)}, u32[]{:S(2)}, u32[]{:S(2)}) %collective-permute-start.1) | collective-permute-done | bytes 135200 | tf_op jit(solution)/shard_map/ppermute | solution.py:314
  64.1 2.9 %constant_dynamic-update-slice_fusion.7 = (bf16[64,512]{1,0:T(8,128)(2,1)S(1)}, bf16[8,512]{1,0:T(8,128)(2,1)S(1)}) fusion(bf16[4096,512]{1,0:T(8,128)(2,1)} %param.19, f32[8,4096]{1,0:T(8,128)S(1)} %fusion.8, f32[8,32]{0,1:T(8,128)S(1)} %copy.125, bf16[8,512]{1,0:T(8,128)(2,1)S(1)} %copy-done.9), kind=kOutput, calls=%fused_computation.53 | convolution fusion | flops 33632256 | bytes 4350976 | tf_op jit(solution)/shard_map/dot_general | solution.py:616
  67.0 13.2 %pack_lines.4.refs_0_ = bf16[8,704,512]{2,1,0:T(8,128)(2,1)S(1)} custom-call(s32[256]{0:T(256)S(1)} %reshape_squeeze.28.plan_ref, s32[8,1,768]{2,1,0:T(1,128)S(1)} %get-tuple-element.9.place_ref, bf16[8,3,704,512]{3,2,1,0:T(8,128)(2,1)} %bitcast.86), custom_call_target="tpu_custom_call" | custom-call | flops 5444206592 | bytes 11534336 | tf_op jit(solution)/shard_map/pack_lines/pallas_call | solution.py:234
  80.2 2.5 copy-done
  86.5 2.5 collective-permute-start.8
  89.0 7.9 %collective-permute-done.4 = bf16[8,512]{1,0:T(8,128)(2,1)S(1)} collective-permute-done((bf16[8,512]{1,0:T(8,128)(2,1)S(1)}, bf16[8,512]{1,0:T(8,128)(2,1)S(1)}, u32[]{:S(2)}, u32[]{:S(2)}) %collective-permute-start.4) | collective-permute-done | bytes 8224 | tf_op jit(solution)/shard_map/ppermute | solution.py:314
  98.1 2.8 %collective-permute-done.9 = bf16[8,512]{1,0:T(8,128)(2,1)S(1)} collective-permute-done((bf16[8,512]{1,0:T(8,128)(2,1)S(1)}, bf16[8,512]{1,0:T(8,128)(2,1)S(1)}, u32[]{:S(2)}, u32[]{:S(2)}) %collective-permute-start.9) | collective-permute-done | bytes 8224 | tf_op jit(solution)/shard_map/ppermute | solution.py:314
  101.5 5.0 %all-to-all-start.1 = ((bf16[8,704,512]{2,1,0:T(8,128)(2,1)}), bf16[8,704,512]{2,1,0:T(8,128)(2,1)}, u32[]{:S(2)}, u32[]{:S(2)}) async-start(bf16[8,704,512]{2,1,0:T(8,128)(2,1)} %after.3), calls=%async_computation.1 | async-start | bytes 11534336 | tf_op jit(solution)/shard_map/all_to_all | solution.py:344
  107.7 8.8 %gate_up.1 = bf16[4,4,16,768]{3,2,1,0:T(8,128)(2,1)S(1)} custom-call(s32[1]{0:T(128)} %bitcast.19.me_ref, bf16[64,512]{1,0:T(8,128)(2,1)S(1)} %copy-done.4, bf16[1,512]{1,0:T(2,128)(2,1)S(1)} %reshape.114.gain_ref, bf16[512,128]{1,0:T(8,128)(2,1)S(1)} %pad.11.router_ref, s32[64,2]{1,0:T(8,128)S(1)} %bitcast.82, bf16[8,3,704,512]{3,2,1,0:T(8,128)(2,1)} %bitcast.87, ...), custom_call_target="tpu_custom_call" | custom-call | flops 738197504 | bytes 11534336 | tf_op jit(solution)/shard_map/gate_up/pallas_call | solution.py:545
  116.5 2.5 collective-permute-start.10
  119.0 2.6 collective-permute-start.11
  122.3 7.4 %collective-permute-done.11.refs_2_ = bf16[4,16,768]{2,1,0:T(8,128)(2,1)S(1)} collective-permute-done((bf16[4,16,768]{2,1,0:T(8,128)(2,1)S(1)}, bf16[4,16,768]{2,1,0:T(8,128)(2,1)S(1)}, u32[]{:S(2)}, u32[]{:S(2)}) %collective-permute-start.11) | collective-permute-done | bytes 98336 | tf_op jit(solution)/shard_map/ppermute | solution.py:314
  134.3 3.5 %collective-permute-done.14.refs_2_ = bf16[2,16,768]{2,1,0:T(8,128)(2,1)S(1)} collective-permute-done((bf16[2,16,768]{2,1,0:T(8,128)(2,1)S(1)}, bf16[2,16,768]{2,1,0:T(8,128)(2,1)S(1)}, u32[]{:S(2)}, u32[]{:S(2)}) %collective-permute-start.14) | collective-permute-done | bytes 49184 | tf_op jit(solution)/shard_map/ppermute | solution.py:314
  139.0 6.1 %down.1 = f32[64,512]{1,0:T(8,128)S(1)} custom-call(s32[1]{0:T(128)} %bitcast.19.me_ref, s32[64,2]{1,0:T(8,128)S(1)} %bitcast.84, bf16[2,16,768]{2,1,0:T(8,128)(2,1)S(1)} %activate.1.refs_0_, bf16[2,16,768]{2,1,0:T(8,128)(2,1)S(1)} %collective-permute-done.13.refs_1_, bf16[2,16,768]{2,1,0:T(8,128)(2,1)S(1)} %collective-permute-done.14.refs_2_, ...), custom_call_target="tpu_custom_call" | custom-call | flops 369098752 | bytes 5767168 | tf_op jit(solution)/shard_map/down/pallas_call | solution.py:572
  149.0 2.6 collective-permute-start.21
  151.6 20.7 %collective-permute-done.17 = f32[8,512]{1,0:T(8,128)S(1)} collective-permute-done((f32[8,512]{1,0:T(8,128)S(1)}, f32[8,512]{1,0:T(8,128)S(1)}, u32[]{:S(2)}, u32[]{:S(2)}) %collective-permute-start.17) | collective-permute-done | bytes 16416 | tf_op jit(solution)/shard_map/ppermute | solution.py:314
  172.7 13.2 %pack_lines.3.refs_0_ = bf16[8,704,512]{2,1,0:T(8,128)(2,1)S(1)} custom-call(s32[256]{0:T(256)S(1)} %reshape_squeeze.28.plan_ref, s32[8,1,768]{2,1,0:T(1,128)S(1)} %get-tuple-element.9.place_ref, bf16[8,3,704,512]{3,2,1,0:T(8,128)(2,1)} %bitcast.90), custom_call_target="tpu_custom_call" | custom-call | flops 5444206592 | bytes 11534336 | tf_op jit(solution)/shard_map/pack_lines/pallas_call | solution.py:234
  185.9 2.5 copy-done.1
  189.1 4.9 %all-to-all-start = ((bf16[8,704,512]{2,1,0:T(8,128)(2,1)}), bf16[8,704,512]{2,1,0:T(8,128)(2,1)}, u32[]{:S(2)}, u32[]{:S(2)}) async-start(bf16[8,704,512]{2,1,0:T(8,128)(2,1)} %after.2), calls=%async_computation | async-start | bytes 11534336 | tf_op jit(solution)/shard_map/all_to_all | solution.py:344
  194.8 9.8 %incoming_plan.1 = (f32[768,128]{1,0:T(8,128)S(1)}, s32[4,64,128]{2,1,0:T(8,128)S(1)}) custom-call(s32[8,5632]{1,0:T(8,128)S(1)} %copy-done.6, s32[8,768]{1,0:T(8,128)S(1)} %pad.12.wanted_ref), custom_call_target="tpu_custom_call" | custom-call | flops 230686720 | bytes 360448 | tf_op jit(solution)/shard_map/incoming_plan/pallas_call | solution.py:218
  204.8 15.7 %unpack_lines.3.rest_0_ = bf16[8,3,704,512]{3,2,1,0:T(8,128)(2,1)} custom-call(s32[256]{0:T(256)S(1)} %reshape_squeeze.27.plan_ref, f32[768,128]{1,0:T(8,128)S(1)} %get-tuple-element.7.place_ref, bf16[8,704,512]{2,1,0:T(8,128)(2,1)} %all-to-all-done.2.block_ref), custom_call_target="tpu_custom_call" | custom-call | flops 5905580032 | bytes 11534336 | tf_op jit(solution)/shard_map/unpack_lines/pallas_call | solution.py:270
  220.5 15.7 %unpack_lines.4.rest_0_ = bf16[8,3,704,512]{3,2,1,0:T(8,128)(2,1)} custom-call(s32[256]{0:T(256)S(1)} %reshape_squeeze.27.plan_ref, f32[768,128]{1,0:T(8,128)S(1)} %get-tuple-element.7.place_ref, bf16[8,704,512]{2,1,0:T(8,128)(2,1)} %all-to-all-done.1.block_ref, bf16[8,3,704,512]{3,2,1,0:T(8,128)(2,1)} %unpack_lines.3.rest_0_), custom_call_target="tpu_custom_call", output_to_operand_aliasing={{}: (3, {})} | custom-call | flops 5905580032 | bytes 11534336 | tf_op jit(solution)/shard_map/unpack_lines/pallas_call | solution.py:270
  236.2 23.7 %all-to-all-done.block_ref = bf16[8,704,512]{2,1,0:T(8,128)(2,1)} async-done(((bf16[8,704,512]{2,1,0:T(8,128)(2,1)}), bf16[8,704,512]{2,1,0:T(8,128)(2,1)}, u32[]{:S(2)}, u32[]{:S(2)}) %all-to-all-start) | async-done | bytes 5767200 | tf_op jit(solution)/shard_map/all_to_all | solution.py:344
  259.9 15.7 %unpack_lines.5 = bf16[8,3,704,512]{3,2,1,0:T(8,128)(2,1)} custom-call(s32[256]{0:T(256)S(1)} %reshape_squeeze.27.plan_ref, f32[768,128]{1,0:T(8,128)S(1)} %get-tuple-element.7.place_ref, bf16[8,704,512]{2,1,0:T(8,128)(2,1)} %all-to-all-done.block_ref, bf16[8,3,704,512]{3,2,1,0:T(8,128)(2,1)} %unpack_lines.4.rest_0_), custom_call_target="tpu_custom_call", output_to_operand_aliasing={{}: (3, {})} | custom-call | flops 5905580032 | bytes 11534336 | tf_op jit(solution)/shard_map/unpack_lines/pallas_call | solution.py:270
  (124 shorter events, 35.3 us)
Async XLA Ops:
  26.2 75.3 %all-to-all-start.2 = ((bf16[8,704,512]{2,1,0:T(8,128)(2,1)}), bf16[8,704,512]{2,1,0:T(8,128)(2,1)}, u32[]{:S(2)}, u32[]{:S(2)}) async-start(bf16[8,704,512]{2,1,0:T(8,128)(2,1)} %copy-done.2), calls=%async_computation.2 | async-start | bytes 11534336 | tf_op jit(solution)/shard_map/all_to_all | solution.py:344
  33.2 6.0 %copy-start.8 = (bf16[8,2,2048]{2,1,0:T(2,128)(2,1)S(1)}, bf16[8,2,2048]{2,1,0:T(2,128)(2,1)}, u32[]{:S(2)}) copy-start(bf16[8,2,2048]{2,1,0:T(2,128)(2,1)} %param.15) | copy-start | bytes 196612
  42.9 21.3 %copy-start.9 = (bf16[8,512]{1,0:T(8,128)(2,1)S(1)}, bf16[8,512]{1,0:T(8,128)(2,1)}, u32[]{:S(2)}) copy-start(bf16[8,512]{1,0:T(8,128)(2,1)} %param.13) | copy-start | bytes 24580
  47.9 8.9 %collective-permute-start = (f32[8,4224]{1,0:T(8,128)S(1)}, f32[8,4224]{1,0:T(8,128)S(1)}, u32[]{:S(2)}, u32[]{:S(2)}) collective-permute-start(f32[8,4224]{1,0:T(8,128)S(1)} %concatenate.6), channel_id=1, source_target_pairs={{0,1},{1,0},{2,3},{3,2},{4,5},{5,4},{6,7},{7,6},{8,9},{9,8},{10,11... | collective-permute-start | bytes 405512 | tf_op jit(solution)/shard_map/ppermute | solution.py:314
  50.4 13.2 %collective-permute-start.1 = (f32[8,4224]{1,0:T(8,128)S(1)}, f32[8,4224]{1,0:T(8,128)S(1)}, u32[]{:S(2)}, u32[]{:S(2)}) collective-permute-start(f32[8,4224]{1,0:T(8,128)S(1)} %concatenate.6), channel_id=1, source_target_pairs={{0,2},{1,3},{2,0},{3,1},{4,6},{5,7},{6,4},{7,5},{8,10},{9,11},{10,... | collective-permute-start | bytes 405512 | tf_op jit(solution)/shard_map/ppermute | solution.py:314
  53.0 10.6 %collective-permute-start.2 = (f32[8,4224]{1,0:T(8,128)S(1)}, f32[8,4224]{1,0:T(8,128)S(1)}, u32[]{:S(2)}, u32[]{:S(2)}) collective-permute-start(f32[8,4224]{1,0:T(8,128)S(1)} %concatenate.6), channel_id=1, source_target_pairs={{0,3},{1,2},{2,1},{3,0},{4,7},{5,6},{6,5},{7,4},{8,11},{9,10},{10,... | collective-permute-start | bytes 405512 | tf_op jit(solution)/shard_map/ppermute | solution.py:314
  67.0 19.4 %collective-permute-start.3 = (bf16[8,512]{1,0:T(8,128)(2,1)S(1)}, bf16[8,512]{1,0:T(8,128)(2,1)S(1)}, u32[]{:S(2)}, u32[]{:S(2)}) collective-permute-start(bf16[8,512]{1,0:T(8,128)(2,1)S(1)} %get-tuple-element.38), channel_id=1, source_target_pairs={{0,4},{4,0},{8,12},{12,8},{16,20},{20,16},{24,28},{28,24},{1,5},{5... | collective-permute-start | bytes 24584 | tf_op jit(solution)/shard_map/ppermute | solution.py:314
  82.7 14.2 %collective-permute-start.4 = (bf16[8,512]{1,0:T(8,128)(2,1)S(1)}, bf16[8,512]{1,0:T(8,128)(2,1)S(1)}, u32[]{:S(2)}, u32[]{:S(2)}) collective-permute-start(bf16[8,512]{1,0:T(8,128)(2,1)S(1)} %get-tuple-element.38), channel_id=1, source_target_pairs={{0,8},{4,12},{8,0},{12,4},{16,24},{20,28},{24,16},{28,20},{1,9},{5... | collective-permute-start | bytes 24584 | tf_op jit(solution)/shard_map/ppermute | solution.py:314
  84.6 12.7 %collective-permute-start.5 = (bf16[8,512]{1,0:T(8,128)(2,1)S(1)}, bf16[8,512]{1,0:T(8,128)(2,1)S(1)}, u32[]{:S(2)}, u32[]{:S(2)}) collective-permute-start(bf16[8,512]{1,0:T(8,128)(2,1)S(1)} %get-tuple-element.38), channel_id=1, source_target_pairs={{0,12},{4,8},{8,4},{12,0},{16,28},{20,24},{24,20},{28,16},{1,13},{... | collective-permute-start | bytes 24584 | tf_op jit(solution)/shard_map/ppermute | solution.py:314
  84.7 12.6 %collective-permute-start.6 = (bf16[8,512]{1,0:T(8,128)(2,1)S(1)}, bf16[8,512]{1,0:T(8,128)(2,1)S(1)}, u32[]{:S(2)}, u32[]{:S(2)}) collective-permute-start(bf16[8,512]{1,0:T(8,128)(2,1)S(1)} %get-tuple-element.38), channel_id=1, source_target_pairs={{0,16},{4,20},{8,24},{12,28},{16,0},{20,4},{24,8},{28,12},{1,17},{... | collective-permute-start | bytes 24584 | tf_op jit(solution)/shard_map/ppermute | solution.py:314
  86.5 11.4 %collective-permute-start.7 = (bf16[8,512]{1,0:T(8,128)(2,1)S(1)}, bf16[8,512]{1,0:T(8,128)(2,1)S(1)}, u32[]{:S(2)}, u32[]{:S(2)}) collective-permute-start(bf16[8,512]{1,0:T(8,128)(2,1)S(1)} %get-tuple-element.38), channel_id=1, source_target_pairs={{0,20},{4,16},{8,28},{12,24},{16,4},{20,0},{24,12},{28,8},{1,21},{... | collective-permute-start | bytes 24584 | tf_op jit(solution)/shard_map/ppermute | solution.py:314
  86.5 11.6 %collective-permute-start.8 = (bf16[8,512]{1,0:T(8,128)(2,1)S(1)}, bf16[8,512]{1,0:T(8,128)(2,1)S(1)}, u32[]{:S(2)}, u32[]{:S(2)}) collective-permute-start(bf16[8,512]{1,0:T(8,128)(2,1)S(1)} %get-tuple-element.38), channel_id=1, source_target_pairs={{0,24},{4,28},{8,16},{12,20},{16,8},{20,12},{24,0},{28,4},{1,25},{... | collective-permute-start | bytes 24584 | tf_op jit(solution)/shard_map/ppermute | solution.py:314
  96.9 4.0 %collective-permute-start.9 = (bf16[8,512]{1,0:T(8,128)(2,1)S(1)}, bf16[8,512]{1,0:T(8,128)(2,1)S(1)}, u32[]{:S(2)}, u32[]{:S(2)}) collective-permute-start(bf16[8,512]{1,0:T(8,128)(2,1)S(1)} %get-tuple-element.38), channel_id=1, source_target_pairs={{0,28},{4,24},{8,20},{12,16},{16,12},{20,8},{24,4},{28,0},{1,29},{... | collective-permute-start | bytes 24584 | tf_op jit(solution)/shard_map/ppermute | solution.py:314
  101.5 5.9 %copy-start.10 = (bf16[512,8]{0,1:T(8,128)(2,1)S(1)}, bf16[512,8]{0,1:T(8,128)(2,1)}, u32[]{:S(2)}) copy-start(bf16[512,8]{0,1:T(8,128)(2,1)} %param.21) | copy-start | bytes 24580
  101.5 6.1 %copy-start.12 = (bf16[512]{0:T(512)(128)(2,1)S(1)}, bf16[512]{0:T(512)(128)(2,1)}, u32[]{:S(2)}) copy-start(bf16[512]{0:T(512)(128)(2,1)} %param.20) | copy-start | bytes 3076
  101.5 6.2 %copy-start.4 = (bf16[64,512]{1,0:T(8,128)(2,1)S(1)}, bf16[64,512]{1,0:T(8,128)(2,1)}, u32[]{:S(2)}) copy-start(bf16[64,512]{1,0:T(8,128)(2,1)} %copy-done.3) | copy-start | bytes 196612
  101.5 87.5 %all-to-all-start.1 = ((bf16[8,704,512]{2,1,0:T(8,128)(2,1)}), bf16[8,704,512]{2,1,0:T(8,128)(2,1)}, u32[]{:S(2)}, u32[]{:S(2)}) async-start(bf16[8,704,512]{2,1,0:T(8,128)(2,1)} %after.3), calls=%async_computation.1 | async-start | bytes 11534336 | tf_op jit(solution)/shard_map/all_to_all | solution.py:344
  116.5 5.8 %collective-permute-start.10 = (bf16[4,16,768]{2,1,0:T(8,128)(2,1)S(1)}, bf16[4,16,768]{2,1,0:T(8,128)(2,1)S(1)}, u32[]{:S(2)}, u32[]{:S(2)}) collective-permute-start(bf16[4,16,768]{2,1,0:T(8,128)(2,1)S(1)} %get-tuple-element.22), channel_id=1, source_target_pairs={{0,1},{1,0},{2,3},{3,2},{4,5},{5,4},{6,7},{7,6},{8,9},{9,8},{10,11... | collective-permute-start | bytes 294920 | tf_op jit(solution)/shard_map/ppermute | solution.py:314
  119.0 10.7 %collective-permute-start.11 = (bf16[4,16,768]{2,1,0:T(8,128)(2,1)S(1)}, bf16[4,16,768]{2,1,0:T(8,128)(2,1)S(1)}, u32[]{:S(2)}, u32[]{:S(2)}) collective-permute-start(bf16[4,16,768]{2,1,0:T(8,128)(2,1)S(1)} %get-tuple-element.21), channel_id=1, source_target_pairs={{0,2},{1,3},{2,0},{3,1},{4,6},{5,7},{6,4},{7,5},{8,10},{9,11},{10,... | collective-permute-start | bytes 294920 | tf_op jit(solution)/shard_map/ppermute | solution.py:314
  121.6 8.1 %collective-permute-start.12 = (bf16[4,16,768]{2,1,0:T(8,128)(2,1)S(1)}, bf16[4,16,768]{2,1,0:T(8,128)(2,1)S(1)}, u32[]{:S(2)}, u32[]{:S(2)}) collective-permute-start(bf16[4,16,768]{2,1,0:T(8,128)(2,1)S(1)} %get-tuple-element.20), channel_id=1, source_target_pairs={{0,3},{1,2},{2,1},{3,0},{4,7},{5,6},{6,5},{7,4},{8,11},{9,10},{10,... | collective-permute-start | bytes 294920 | tf_op jit(solution)/shard_map/ppermute | solution.py:314
  129.9 4.5 %collective-permute-start.13 = (bf16[2,16,768]{2,1,0:T(8,128)(2,1)S(1)}, bf16[2,16,768]{2,1,0:T(8,128)(2,1)S(1)}, u32[]{:S(2)}, u32[]{:S(2)}) collective-permute-start(bf16[2,16,768]{2,1,0:T(8,128)(2,1)S(1)} %activate.1.refs_0_), channel_id=1, source_target_pairs={{0,1},{1,0},{2,3},{3,2},{4,5},{5,4},{6,7},{7,6},{8,9},{9,8},{10,11... | collective-permute-start | bytes 147464 | tf_op jit(solution)/shard_map/ppermute | solution.py:314
  131.8 6.0 %collective-permute-start.14 = (bf16[2,16,768]{2,1,0:T(8,128)(2,1)S(1)}, bf16[2,16,768]{2,1,0:T(8,128)(2,1)S(1)}, u32[]{:S(2)}, u32[]{:S(2)}) collective-permute-start(bf16[2,16,768]{2,1,0:T(8,128)(2,1)S(1)} %activate.1.refs_0_), channel_id=1, source_target_pairs={{0,2},{1,3},{2,0},{3,1},{4,6},{5,7},{6,4},{7,5},{8,10},{9,11},{10,... | collective-permute-start | bytes 147464 | tf_op jit(solution)/shard_map/ppermute | solution.py:314
  133.1 5.9 %collective-permute-start.15 = (bf16[2,16,768]{2,1,0:T(8,128)(2,1)S(1)}, bf16[2,16,768]{2,1,0:T(8,128)(2,1)S(1)}, u32[]{:S(2)}, u32[]{:S(2)}) collective-permute-start(bf16[2,16,768]{2,1,0:T(8,128)(2,1)S(1)} %activate.1.refs_0_), channel_id=1, source_target_pairs={{0,3},{1,2},{2,1},{3,0},{4,7},{5,6},{6,5},{7,4},{8,11},{9,10},{10,... | collective-permute-start | bytes 147464 | tf_op jit(solution)/shard_map/ppermute | solution.py:314
  145.1 3.8 %collective-permute-start.16 = (f32[8,512]{1,0:T(8,128)S(1)}, f32[8,512]{1,0:T(8,128)S(1)}, u32[]{:S(2)}, u32[]{:S(2)}) collective-permute-start(f32[8,512]{1,0:T(8,128)S(1)} %get-tuple-element.24), channel_id=1, source_target_pairs={{0,4},{4,0},{8,12},{12,8},{16,20},{20,16},{24,28},{28,24},{1,5},{5... | collective-permute-start | bytes 49160 | tf_op jit(solution)/shard_map/ppermute | solution.py:314
  145.2 27.0 %collective-permute-start.17 = (f32[8,512]{1,0:T(8,128)S(1)}, f32[8,512]{1,0:T(8,128)S(1)}, u32[]{:S(2)}, u32[]{:S(2)}) collective-permute-start(f32[8,512]{1,0:T(8,128)S(1)} %get-tuple-element.30), channel_id=1, source_target_pairs={{0,8},{4,12},{8,0},{12,4},{16,24},{20,28},{24,16},{28,20},{1,9},{5... | collective-permute-start | bytes 49160 | tf_op jit(solution)/shard_map/ppermute | solution.py:314
  147.1 41.3 %collective-permute-start.18 = (f32[8,512]{1,0:T(8,128)S(1)}, f32[8,512]{1,0:T(8,128)S(1)}, u32[]{:S(2)}, u32[]{:S(2)}) collective-permute-start(f32[8,512]{1,0:T(8,128)S(1)} %get-tuple-element.29), channel_id=1, source_target_pairs={{0,12},{4,8},{8,4},{12,0},{16,28},{20,24},{24,20},{28,16},{1,13},{... | collective-permute-start | bytes 49160 | tf_op jit(solution)/shard_map/ppermute | solution.py:314
  147.2 41.2 %collective-permute-start.19 = (f32[8,512]{1,0:T(8,128)S(1)}, f32[8,512]{1,0:T(8,128)S(1)}, u32[]{:S(2)}, u32[]{:S(2)}) collective-permute-start(f32[8,512]{1,0:T(8,128)S(1)} %get-tuple-element.28), channel_id=1, source_target_pairs={{0,16},{4,20},{8,24},{12,28},{16,0},{20,4},{24,8},{28,12},{1,17},{... | collective-permute-start | bytes 49160 | tf_op jit(solution)/shard_map/ppermute | solution.py:314
  149.0 39.4 %collective-permute-start.20 = (f32[8,512]{1,0:T(8,128)S(1)}, f32[8,512]{1,0:T(8,128)S(1)}, u32[]{:S(2)}, u32[]{:S(2)}) collective-permute-start(f32[8,512]{1,0:T(8,128)S(1)} %get-tuple-element.27), channel_id=1, source_target_pairs={{0,20},{4,16},{8,28},{12,24},{16,4},{20,0},{24,12},{28,8},{1,21},{... | collective-permute-start | bytes 49160 | tf_op jit(solution)/shard_map/ppermute | solution.py:314
  149.0 39.4 %collective-permute-start.21 = (f32[8,512]{1,0:T(8,128)S(1)}, f32[8,512]{1,0:T(8,128)S(1)}, u32[]{:S(2)}, u32[]{:S(2)}) collective-permute-start(f32[8,512]{1,0:T(8,128)S(1)} %get-tuple-element.26), channel_id=1, source_target_pairs={{0,24},{4,28},{8,16},{12,20},{16,8},{20,12},{24,0},{28,4},{1,25},{... | collective-permute-start | bytes 49160 | tf_op jit(solution)/shard_map/ppermute | solution.py:314
  172.2 16.2 %collective-permute-start.22 = (f32[8,512]{1,0:T(8,128)S(1)}, f32[8,512]{1,0:T(8,128)S(1)}, u32[]{:S(2)}, u32[]{:S(2)}) collective-permute-start(f32[8,512]{1,0:T(8,128)S(1)} %get-tuple-element.25), channel_id=1, source_target_pairs={{0,28},{4,24},{8,20},{12,16},{16,12},{20,8},{24,4},{28,0},{1,29},{... | collective-permute-start | bytes 49160 | tf_op jit(solution)/shard_map/ppermute | solution.py:314
  189.1 5.7 %copy-start.6 = (s32[8,5632]{1,0:T(8,128)S(1)}, s32[8,5632]{1,0:T(8,128)}, u32[]{:S(2)}) copy-start(s32[8,5632]{1,0:T(8,128)} %old_ref.1) | copy-start | bytes 540676
  189.1 70.8 %all-to-all-start = ((bf16[8,704,512]{2,1,0:T(8,128)(2,1)}), bf16[8,704,512]{2,1,0:T(8,128)(2,1)}, u32[]{:S(2)}, u32[]{:S(2)}) async-start(bf16[8,704,512]{2,1,0:T(8,128)(2,1)} %after.2), calls=%async_computation | async-start | bytes 11534336 | tf_op jit(solution)/shard_map/all_to_all | solution.py:344
  (8 other events, 23.6 us)
